TPU v7x, 512 devices: a whole 4x8x8 slice. The times are simulated.
512 devices in a mesh: ctx: 64 (over x, y, core), ch: 8 (over z).
Axes of the slice: x: 4, y: 8, z: 8, core: 2. Of those that a mesh axis runs over, the one named last changes fastest.
Arguments:
- outer_gate: bfloat16 [256, 16384], P('ch', 'ctx'), may hold values from -6 to 6
- inner_gate: bfloat16 [256, 16384], P('ch', 'ctx'), may hold values from -6 to 6
- values: bfloat16 [256, 16384], P('ch', 'ctx'), may hold values from -6 to 6
- grad_out: bfloat16 [256, 16384], P('ch', 'ctx'), may hold values from -6 to 6
- long_filter: float32 [32, 16384], P(None, 'ctx'), may hold values from -1 to 1
- mid_filter: float32 [256, 128], P('ch'), may hold values from -0.5 to 0.5
Outputs:
- grad_outer_gate: bfloat16 [256, 16384], P('ch', 'ctx')
- grad_inner_gate: bfloat16 [256, 16384], P('ch', 'ctx')
- grad_values: bfloat16 [256, 16384], P('ch', 'ctx')
- grad_long: float32 [32, 16384], P('ch', 'ctx')
- grad_mid: float32 [256, 128], P('ch')
All inputs are finite; a program needn't handle non-finite values.
Results may differ from a plain program's by a relative error of at most 0.0029.
Values sent between devices are 32-bit elements; how exact they have to be, the bound alone decides.
A program may use at most 64 MiB of HBM per device.

v0:
```python
import math

import jax
import jax.numpy as jnp
from jax import lax
from jax.sharding import PartitionSpec as P

two_pi = 2.0 * math.pi
highest = lax.Precision.HIGHEST
lane_width = 128


def from_behind(shard, axis, by):
    size = lax.axis_size(axis)
    pairs = [(i, i + by) for i in range(size) if 0 <= i + by < size]
    return lax.ppermute(shard, axis, pairs)


def phases(products, period):
    angles = (products % period).astype(jnp.float32) * (two_pi / period)
    return (jnp.cos(angles), jnp.sin(angles))


def contract(form, cos_table, sin_table, real_part, imag_part, sign):
    cos_real = jnp.einsum(form, cos_table, real_part, precision=highest)
    sin_imag = jnp.einsum(form, sin_table, imag_part, precision=highest)
    cos_imag = jnp.einsum(form, cos_table, imag_part, precision=highest)
    sin_real = jnp.einsum(form, sin_table, real_part, precision=highest)
    return (cos_real - sign * sin_imag, cos_imag + sign * sin_real)


def rotate(real_part, imag_part, cos_table, sin_table, sign):
    return (
        real_part * cos_table - sign * imag_part * sin_table,
        imag_part * cos_table + sign * real_part * sin_table,
    )


def local_tables(tok_rows):
    outer_len = tok_rows // lane_width
    outer_idx = jnp.arange(outer_len, dtype=jnp.int32)
    inner_idx = jnp.arange(lane_width, dtype=jnp.int32)
    outer_cs = phases(outer_idx[:, None] * outer_idx[None, :], outer_len)
    twist_cs = phases(outer_idx[:, None] * inner_idx[None, :], tok_rows)
    inner_cs = phases(inner_idx[:, None] * inner_idx[None, :], lane_width)
    return (outer_cs, twist_cs, inner_cs)


def expand(table):
    return table[None, None, :, :, None]


def spectrum(fields):
    field_count, tok_rows, ch_width = fields.shape
    ctx_count = lax.axis_size("ctx")
    my_index = lax.axis_index("ctx")
    row_block = tok_rows // ctx_count
    padded_len = 2 * ctx_count * tok_rows
    spread = lax.all_to_all(
        fields.reshape(field_count, ctx_count, row_block * ch_width),
        "ctx",
        split_axis=1,
        concat_axis=1,
        tiled=True,
    )
    device_idx = jnp.arange(ctx_count, dtype=jnp.int32)
    coarse_idx = jnp.arange(2 * ctx_count, dtype=jnp.int32)
    coarse_cos, coarse_sin = phases(coarse_idx[:, None] * device_idx[None, :], 2 * ctx_count)
    real_part = jnp.einsum("an,knm->kam", coarse_cos, spread, precision=highest)
    imag_part = -jnp.einsum("an,knm->kam", coarse_sin, spread, precision=highest)
    block_shape = (field_count, 2 * ctx_count, row_block, ch_width)
    row_idx = my_index * row_block + jnp.arange(row_block, dtype=jnp.int32)
    twist_cos, twist_sin = phases(coarse_idx[:, None] * row_idx[None, :], padded_len)
    real_part, imag_part = rotate(
        real_part.reshape(block_shape),
        imag_part.reshape(block_shape),
        twist_cos[None, :, :, None],
        twist_sin[None, :, :, None],
        -1.0,
    )
    stacked = jnp.stack([real_part, imag_part], 1).reshape(
        field_count, 2, 2 * ctx_count, row_block * ch_width
    )
    arrived = lax.all_to_all(stacked, "ctx", split_axis=2, concat_axis=3, tiled=True)
    arrived = arrived.reshape(field_count, 2, 2, tok_rows // lane_width, lane_width, ch_width)
    real_part, imag_part = (arrived[:, 0], arrived[:, 1])
    outer_cs, twist_cs, inner_cs = local_tables(tok_rows)
    real_part, imag_part = contract(
        "bp,kapqc->kabqc", outer_cs[0], outer_cs[1], real_part, imag_part, -1.0
    )
    real_part, imag_part = rotate(
        real_part, imag_part, expand(twist_cs[0]), expand(twist_cs[1]), -1.0
    )
    return contract("eq,kabqc->kabec", inner_cs[0], inner_cs[1], real_part, imag_part, -1.0)


def time_field(real_part, imag_part):
    field_count = real_part.shape[0]
    tok_rows = real_part.shape[2] * lane_width
    ch_width = real_part.shape[4]
    ctx_count = lax.axis_size("ctx")
    my_index = lax.axis_index("ctx")
    padded_len = 2 * ctx_count * tok_rows
    outer_cs, twist_cs, inner_cs = local_tables(tok_rows)
    real_part, imag_part = contract(
        "qe,kabec->kabqc", inner_cs[0], inner_cs[1], real_part, imag_part, 1.0
    )
    real_part, imag_part = rotate(
        real_part, imag_part, expand(twist_cs[0]), expand(twist_cs[1]), 1.0
    )
    real_part, imag_part = contract(
        "pb,kabqc->kapqc", outer_cs[0], outer_cs[1], real_part, imag_part, 1.0
    )
    real_part = real_part.reshape(field_count, 2, tok_rows, ch_width)
    imag_part = imag_part.reshape(field_count, 2, tok_rows, ch_width)
    row_idx = jnp.arange(tok_rows, dtype=jnp.int32)
    device_idx = jnp.arange(ctx_count, dtype=jnp.int32)
    pair_idx = my_index * 2 + jnp.arange(2, dtype=jnp.int32)
    twist_cos, twist_sin = phases(pair_idx[:, None] * row_idx[None, :], padded_len)
    real_part, imag_part = rotate(
        real_part, imag_part, twist_cos[None, :, :, None], twist_sin[None, :, :, None], 1.0
    )
    stacked = jnp.stack([real_part, imag_part], 1).reshape(field_count, 2, 2, tok_rows * ch_width)
    returned = lax.all_to_all(stacked, "ctx", split_axis=3, concat_axis=2, tiled=True)
    coarse_idx = jnp.arange(2 * ctx_count, dtype=jnp.int32)
    coarse_cos, coarse_sin = phases(device_idx[:, None] * coarse_idx[None, :], 2 * ctx_count)
    result = (
        jnp.einsum("na,kam->knm", coarse_cos, returned[:, 0], precision=highest)
        - jnp.einsum("na,kam->knm", coarse_sin, returned[:, 1], precision=highest)
    ) / padded_len
    settled = lax.all_to_all(result, "ctx", split_axis=1, concat_axis=1, tiled=True)
    return settled.reshape(field_count, tok_rows, ch_width)


def depthwise(signal, filter_taps):
    ch_width = signal.shape[1]
    output = lax.conv_general_dilated(
        signal[None],
        filter_taps[:, None, :],
        (1,),
        "VALID",
        dimension_numbers=("NWC", "WIO", "NWC"),
        feature_group_count=ch_width,
        precision=highest,
    )
    return output[0]


def local(outer_gate, inner_gate, values, grad_out, long_filter, mid_filter):
    outer_gate = outer_gate.T
    inner_gate = inner_gate.T
    values = values.T
    grad_out = grad_out.T
    long_filter = long_filter.T
    mid_filter = mid_filter.T
    tok_rows, ch_width = values.shape
    reach_rows = mid_filter.shape[0] - 1
    ctx_count = lax.axis_size("ctx")
    norm_scale = (tok_rows * ctx_count) ** (-0.5)
    product = inner_gate.astype(jnp.float32) * values.astype(jnp.float32)
    earlier = from_behind(product[tok_rows - reach_rows :], "ctx", 1)
    extended = jnp.concatenate([earlier, product], 0)
    mixed = depthwise(extended, mid_filter[::-1])
    both_re, both_im = spectrum(jnp.stack([mixed, long_filter], 0))
    mix_re, mix_im, filt_re, filt_im = (both_re[0], both_im[0], both_re[1], both_im[1])
    signal_re = mix_re * filt_re - mix_im * filt_im
    signal_im = mix_re * filt_im + mix_im * filt_re
    recon_field = time_field(signal_re[None], signal_im[None])[0]
    grad_full = grad_out.astype(jnp.float32)
    grad_outer = (grad_full * recon_field).astype(jnp.bfloat16)
    grad_conv = grad_full * outer_gate.astype(jnp.float32)
    cot_re, cot_im = spectrum(grad_conv[None])
    cot_re, cot_im = (cot_re[0], cot_im[0])
    back_re = cot_re * filt_re + cot_im * filt_im
    back_im = cot_im * filt_re - cot_re * filt_im
    tap_re = cot_re * mix_re + cot_im * mix_im
    tap_im = cot_im * mix_re - cot_re * mix_im
    both_fields = time_field(jnp.stack([back_re, tap_re], 0), jnp.stack([back_im, tap_im], 0))
    grad_mixed = both_fields[0]
    grad_long = lax.psum_scatter(both_fields[1], "ch", scatter_dimension=1, tiled=True) * norm_scale
    later_rows = from_behind(grad_mixed[:reach_rows], "ctx", -1)
    grad_product = depthwise(jnp.concatenate([grad_mixed, later_rows], 0), mid_filter)
    partial_mid = depthwise(extended, grad_mixed)[::-1]
    grad_mid = lax.psum(partial_mid, "ctx") * norm_scale
    grad_inner = (grad_product * values.astype(jnp.float32)).astype(jnp.bfloat16)
    grad_values = (grad_product * inner_gate.astype(jnp.float32)).astype(jnp.bfloat16)
    return (grad_outer.T, grad_inner.T, grad_values.T, grad_long.T, grad_mid.T)


def solution(mesh):
    in_specs = (
        P("ch", "ctx"),
        P("ch", "ctx"),
        P("ch", "ctx"),
        P("ch", "ctx"),
        P(None, "ctx"),
        P("ch", None),
    )
    out_specs = (P("ch", "ctx"), P("ch", "ctx"), P("ch", "ctx"), P("ch", "ctx"), P("ch", None))
    return jax.shard_map(local, mesh=mesh, in_specs=in_specs, out_specs=out_specs, check_vma=False)
```

profile of v0, /device:TPU:1, one launch (start us, length us, event | category | flops | bytes accessed | tf_op | source)
XLA Modules:
  0.0 566.4 jit_solution(7712723140318516772)
XLA Ops:
  0.6 0.7 bitcast_multiply_fusion.2
  1.5 0.7 reshape_broadcast_in_dim.3
  2.2 11.6 %all-to-all-start.4 = ((f32[1,64,128]{2,0,1:T(1,128)}), f32[1,64,128]{2,0,1:T(1,128)S(1)}, u32[]{:S(2)}, u32[]{:S(2)}) async-start(f32[1,64,128]{2,0,1:T(1,128)} %bitcast.72), calls=%async_computation.4 | async-start | bytes 65536 | tf_op jit(solution)/shard_map/all_to_all | solution.py:59
  13.8 0.7 bitcast_multiply_fusion.3
  14.6 3.5 collective-permute-start
  19.5 0.9 copy.150
  20.5 0.8 rev.6
  21.6 2.2 convolution_reduce_fusion
  23.9 0.7 copy.151
  24.6 9.9 %all-to-all-start = ((f32[2,64,128]{2,0,1:T(2,128)}), f32[2,64,128]{2,0,1:T(2,128)S(1)}, u32[]{:S(2)}, u32[]{:S(2)}) async-start(f32[2,64,128]{2,0,1:T(2,128)} %copy.151), calls=%async_computation | async-start | bytes 131072 | tf_op jit(solution)/shard_map/all_to_all | solution.py:59
  35.2 0.8 copy.175
  36.0 8.3 %all-to-all-done = f32[2,64,128]{2,0,1:T(2,128)S(1)} async-done(((f32[2,64,128]{2,0,1:T(2,128)}), f32[2,64,128]{2,0,1:T(2,128)S(1)}, u32[]{:S(2)}, u32[]{:S(2)}) %all-to-all-start) | async-done | bytes 65568 | tf_op jit(solution)/shard_map/all_to_all | solution.py:59
  44.3 4.4 all-to-all-start.5
  49.6 0.8 copy.154
  50.4 8.7 %all-to-all-done.5 = f32[1,2,128,128]{3,1,0,2:T(2,128)S(1)} async-done(((f32[1,2,128,128]{3,1,0,2:T(2,128)}), f32[1,2,128,128]{3,1,0,2:T(2,128)S(1)}, u32[]{:S(2)}, u32[]{:S(2)}) %all-to-all-start.5) | async-done | bytes 131104 | tf_op jit(solution)/shard_map/all_to_all | solution.py:84
  59.2 5.5 all-to-all-start.1
  67.3 0.5 fusion.14
  68.3 8.2 %all-to-all-done.1 = f32[2,2,128,128]{3,0,1,2:T(2,128)S(1)} async-done(((f32[2,2,128,128]{3,0,1,2:T(2,128)}), f32[2,2,128,128]{3,0,1,2:T(2,128)S(1)}, u32[]{:S(2)}, u32[]{:S(2)}) %all-to-all-start.1) | async-done | bytes 262176 | tf_op jit(solution)/shard_map/all_to_all | solution.py:84
  77.1 0.6 fusion.27
  77.9 0.6 fusion.31
  78.5 0.6 fusion.5
  79.1 0.7 multiply_add_fusion.1
  79.8 0.5 convolution_multiply_fusion
  80.4 0.5 convolution_multiply_fusion.1
  81.4 0.5 fusion.1
  81.9 0.5 multiply_add_fusion.3
  84.0 0.5 add_bitcast_fusion.3
  86.9 7.9 %copy.169 = f32[1,2,2,8192]{2,1,0,3:T(2,128)} copy(f32[1,2,2,8192]{3,2,1,0:T(2,128)S(1)} %pad_maximum_fusion.2) | data formatting | bytes 262144 | tf_op jit(solution)/shard_map/stack | solution.py:123
  94.8 14.2 %reshape.571 = f32[64,1,512]{2,1,0:T(1,128)} reshape(f32[8192,1,2,2]{3,2,1,0:T(2,128)} %bitcast.350) | data formatting | bytes 262144
  108.9 6.0 %all-to-all-start.2 = ((f32[64,1,512]{2,1,0:T(1,128)}), f32[64,1,512]{2,1,0:T(1,128)S(1)}, u32[]{:S(2)}, u32[]{:S(2)}) async-start(f32[64,1,512]{2,1,0:T(1,128)} %reshape.571), calls=%async_computation.2 | async-start | bytes 262144 | tf_op jit(solution)/shard_map/all_to_all | solution.py:124
  116.0 0.5 convolution_add_fusion
  116.5 0.5 add_bitcast_fusion
  117.0 0.6 fusion.39
  117.7 0.6 fusion.43
  118.3 0.6 fusion.2
  119.5 0.6 fusion.3
  120.8 4.5 all-to-all-done.2
  125.8 0.9 reduce.18
  126.8 14.2 %reshape.572 = f32[8192,1,2,2]{3,2,1,0:T(2,128)} reshape(f32[64,512]{1,0:T(8,128)S(1)} %reduce.18) | data formatting | bytes 262144
  141.0 9.3 %copy.170 = f32[1,2,2,64,128]{4,2,3,1,0:T(2,128)S(1)} copy(f32[1,2,2,64,128]{2,1,4,3,0:T(2,128)} %bitcast.351) | data formatting | bytes 262144 | tf_op jit(solution)/shard_map/all_to_all | solution.py:124
  150.6 0.9 fusion.24
  151.6 5.8 %all-to-all-start.3 = ((f32[1,64,128]{2,0,1:T(1,128)}), f32[1,64,128]{2,0,1:T(1,128)S(1)}, u32[]{:S(2)}, u32[]{:S(2)}) async-start(f32[1,64,128]{2,0,1:T(1,128)} %bitcast.69), calls=%async_computation.3 | async-start | bytes 65536 | tf_op jit(solution)/shard_map/all_to_all | solution.py:131
  157.5 15.3 %copy.190 = f32[2,2,2,8192]{2,0,1,3:T(2,128)} copy(f32[2,2,2,8192]{3,2,0,1:T(2,128)S(1)} %pad_maximum_fusion.1) | data formatting | bytes 524288 | tf_op jit(solution)/shard_map/stack | solution.py:123
  172.8 25.8 %reshape.573 = f32[64,1,1024]{2,1,0:T(1,128)} reshape(f32[8192,2,2,2]{3,2,1,0:T(2,128)} %bitcast.348) | data formatting | bytes 524288
  198.6 10.3 %all-to-all-start.6 = ((f32[64,1,1024]{2,1,0:T(1,128)}), f32[64,1,1024]{2,1,0:T(1,128)S(1)}, u32[]{:S(2)}, u32[]{:S(2)}) async-start(f32[64,1,1024]{2,1,0:T(1,128)} %reshape.573), calls=%async_computation.6 | async-start | bytes 524288 | tf_op jit(solution)/shard_map/all_to_all | solution.py:124
  209.1 1.3 dynamic-slice
  211.0 0.5 broadcast.698
  211.5 0.7 reduce.17
  212.4 8.6 %all-to-all-done.6 = f32[64,1,1024]{2,1,0:T(1,128)S(1)} async-done(((f32[64,1,1024]{2,1,0:T(1,128)}), f32[64,1,1024]{2,1,0:T(1,128)S(1)}, u32[]{:S(2)}, u32[]{:S(2)}) %all-to-all-start.6) | async-done | bytes 262176 | tf_op jit(solution)/shard_map/all_to_all | solution.py:124
  221.0 1.3 reduce.19
  222.3 27.0 %reshape.574 = f32[8192,2,2,2]{3,2,1,0:T(2,128)} reshape(f32[64,1024]{1,0:T(8,128)S(1)} %reduce.19) | data formatting | bytes 524288
  249.3 13.4 %copy.211 = f32[2,2,2,64,128]{4,3,2,1,0:T(8,128)S(1)} copy(f32[2,2,2,64,128]{2,0,1,4,3:T(2,128)} %bitcast.349) | data formatting | bytes 524288 | tf_op jit(solution)/shard_map/all_to_all | solution.py:124
  263.6 0.7 copy.193
  264.3 6.0 %all-to-all-start.7 = ((f32[2,64,128]{2,0,1:T(2,128)}), f32[2,64,128]{2,0,1:T(2,128)S(1)}, u32[]{:S(2)}, u32[]{:S(2)}) async-start(f32[2,64,128]{2,0,1:T(2,128)} %copy.193), calls=%async_computation.7 | async-start | bytes 131072 | tf_op jit(solution)/shard_map/all_to_all | solution.py:131
  270.3 0.6 fusion.131
  270.9 9.2 %all-to-all-done.7 = f32[2,64,128]{2,0,1:T(2,128)S(1)} async-done(((f32[2,64,128]{2,0,1:T(2,128)}), f32[2,64,128]{2,0,1:T(2,128)S(1)}, u32[]{:S(2)}, u32[]{:S(2)}) %all-to-all-start.7) | async-done | bytes 65568 | tf_op jit(solution)/shard_map/all_to_all | solution.py:131
  280.4 2.3 collective-permute-start.1
  282.8 30.1 %all-reduce = f32[256,32]{1,0:T(8,128)S(1)} all-reduce(f32[256,32]{1,0:T(8,128)S(1)} %squeeze.40), channel_id=2, replica_groups=mesh['ctx'=64,'ch'=8] {'ch'}, use_global_device_ids=true, to_apply=%region_0.1.clone | all-reduce | flops 8192 | bytes 65536
  313.0 2.4 fusion.378
  315.4 247.0 %psum.7 = f32[128,32]{1,0:T(8,128)S(1)} all-reduce(f32[128,32]{1,0:T(8,128)S(1)} %rev.7), channel_id=1, replica_groups=mesh['ctx'=64,'ch'=8] {'ctx'}, use_global_device_ids=true, to_apply=%region_1.2 | all-reduce | flops 4096 | bytes 32768 | tf_op jit(solution)/shard_map/psum | solution.py:184
  562.5 0.7 copy.201
  563.2 0.7 copy.202
  564.1 1.3 fusion.377
  565.6 0.6 fusion.132
  (101 shorter events, 16.9 us)
Async XLA Ops:
  2.2 22.4 %all-to-all-start.4 = ((f32[1,64,128]{2,0,1:T(1,128)}), f32[1,64,128]{2,0,1:T(1,128)S(1)}, u32[]{:S(2)}, u32[]{:S(2)}) async-start(f32[1,64,128]{2,0,1:T(1,128)} %bitcast.72), calls=%async_computation.4 | async-start | bytes 65536 | tf_op jit(solution)/shard_map/all_to_all | solution.py:59
  14.6 6.7 %collective-permute-start = (f32[127,32]{0,1:T(8,128)S(1)}, f32[127,32]{0,1:T(8,128)S(1)}, u32[]{:S(2)}, u32[]{:S(2)}) collective-permute-start(f32[127,32]{0,1:T(8,128)S(1)} %slice.66), channel_id=1, source_target_pairs={{0,8},{8,16},{16,24},{24,32},{32,40},{40,48},{48,56},{56,64},{64,7... | collective-permute-start | bytes 48776 | tf_op jit(solution)/shard_map/ppermute | solution.py:16
  24.6 19.7 %all-to-all-start = ((f32[2,64,128]{2,0,1:T(2,128)}), f32[2,64,128]{2,0,1:T(2,128)S(1)}, u32[]{:S(2)}, u32[]{:S(2)}) async-start(f32[2,64,128]{2,0,1:T(2,128)} %copy.151), calls=%async_computation | async-start | bytes 131072 | tf_op jit(solution)/shard_map/all_to_all | solution.py:59
  44.3 14.9 %all-to-all-start.5 = ((f32[1,2,128,128]{3,1,0,2:T(2,128)}), f32[1,2,128,128]{3,1,0,2:T(2,128)S(1)}, u32[]{:S(2)}, u32[]{:S(2)}) async-start(f32[1,2,128,128]{3,1,0,2:T(2,128)} %copy.175), calls=%async_computation.5 | async-start | bytes 262144 | tf_op jit(solution)/shard_map/all_to_all | solution.py:84
  59.2 17.3 %all-to-all-start.1 = ((f32[2,2,128,128]{3,0,1,2:T(2,128)}), f32[2,2,128,128]{3,0,1,2:T(2,128)S(1)}, u32[]{:S(2)}, u32[]{:S(2)}) async-start(f32[2,2,128,128]{3,0,1,2:T(2,128)} %copy.154), calls=%async_computation.1 | async-start | bytes 524288 | tf_op jit(solution)/shard_map/all_to_all | solution.py:84
  108.9 16.4 %all-to-all-start.2 = ((f32[64,1,512]{2,1,0:T(1,128)}), f32[64,1,512]{2,1,0:T(1,128)S(1)}, u32[]{:S(2)}, u32[]{:S(2)}) async-start(f32[64,1,512]{2,1,0:T(1,128)} %reshape.571), calls=%async_computation.2 | async-start | bytes 262144 | tf_op jit(solution)/shard_map/all_to_all | solution.py:124
  151.6 47.1 %all-to-all-start.3 = ((f32[1,64,128]{2,0,1:T(1,128)}), f32[1,64,128]{2,0,1:T(1,128)S(1)}, u32[]{:S(2)}, u32[]{:S(2)}) async-start(f32[1,64,128]{2,0,1:T(1,128)} %bitcast.69), calls=%async_computation.3 | async-start | bytes 65536 | tf_op jit(solution)/shard_map/all_to_all | solution.py:131
  157.5 51.5 %copy-start = (f32[32,128]{1,0:T(8,128)S(1)}, f32[32,128]{1,0:T(8,128)}, u32[]{:S(2)}) copy-start(f32[32,128]{1,0:T(8,128)} %param.11) | copy-start | bytes 49156
  198.6 22.3 %all-to-all-start.6 = ((f32[64,1,1024]{2,1,0:T(1,128)}), f32[64,1,1024]{2,1,0:T(1,128)S(1)}, u32[]{:S(2)}, u32[]{:S(2)}) async-start(f32[64,1,1024]{2,1,0:T(1,128)} %reshape.573), calls=%async_computation.6 | async-start | bytes 524288 | tf_op jit(solution)/shard_map/all_to_all | solution.py:124
  222.2 48.1 %copy-start.1 = (bf16[32,256]{1,0:T(8,128)(2,1)S(1)}, bf16[32,256]{1,0:T(8,128)(2,1)}, u32[]{:S(2)}) copy-start(bf16[32,256]{1,0:T(8,128)(2,1)} %param.9) | copy-start | bytes 49156
  249.3 316.3 %copy-start.2 = (bf16[32,256]{1,0:T(8,128)(2,1)S(1)}, bf16[32,256]{1,0:T(8,128)(2,1)}, u32[]{:S(2)}) copy-start(bf16[32,256]{1,0:T(8,128)(2,1)} %param.8) | copy-start | bytes 49156
  249.3 316.3 %copy-start.3 = (bf16[32,256]{1,0:T(8,128)(2,1)S(1)}, bf16[32,256]{1,0:T(8,128)(2,1)}, u32[]{:S(2)}) copy-start(bf16[32,256]{1,0:T(8,128)(2,1)} %param.7) | copy-start | bytes 49156
  264.3 15.8 %all-to-all-start.7 = ((f32[2,64,128]{2,0,1:T(2,128)}), f32[2,64,128]{2,0,1:T(2,128)S(1)}, u32[]{:S(2)}, u32[]{:S(2)}) async-start(f32[2,64,128]{2,0,1:T(2,128)} %copy.193), calls=%async_computation.7 | async-start | bytes 131072 | tf_op jit(solution)/shard_map/all_to_all | solution.py:131
  280.4 283.5 %collective-permute-start.1 = (f32[127,32]{1,0:T(8,128)S(1)}, f32[127,32]{1,0:T(8,128)S(1)}, u32[]{:S(2)}, u32[]{:S(2)}) collective-permute-start(f32[127,32]{1,0:T(8,128)S(1)} %slice.80), channel_id=1, source_target_pairs={{8,0},{16,8},{24,16},{32,24},{40,32},{48,40},{56,48},{64,56},{72,6... | collective-permute-start | bytes 48776 | tf_op jit(solution)/shard_map/ppermute | solution.py:16
where the time goes:
time: 574 us; the launch traced here: 566 us
  blocking collectives  277 us (48%)
  local copies, waits for them, and re-layouts  142 us (25%)
  starting transfers between devices  65.4 us (11%)
  waiting for transfers between devices  47.5 us (8%)
  matrix products  26 us (5%)
  other arithmetic  6.6 us (1%)
    psum x1, blocking collectives, local(): grad_mid = lax.psum(partial_mid, 'ctx') * norm_scale  247 us
    unnamed x19, local copies, waits for them, and re-layouts  84.5 us
    unnamed x1, blocking collectives  30.1 us
    all_to_all x4, local copies, waits for them, and re-layouts, time_field(): lax.all_to_all(stacked, 'ctx', split_axis=3, concat_axis=2, tiled=True)  23.4 us
    another operation x2, local copies, waits for them, and re-layouts, time_field(): jnp.stack([real_part, imag_part], 1)  23.2 us
    all_to_all x2, starting transfers between devices, spectrum(): lax.all_to_all(fields.reshape(field_count, ctx_count, row_block * ch_widt...  21.5 us
    all_to_all x2, waiting for transfers between devices, spectrum(): lax.all_to_all(stacked, 'ctx', split_axis=2, concat_axis=3, tiled=True)  16.9 us
    all_to_all x2, starting transfers between devices, time_field(): lax.all_to_all(stacked, 'ctx', split_axis=3, concat_axis=2, tiled=True)  16.3 us
  transfers between devices with their start and end apart: 10, of which 6 were waited for; matrix products, arithmetic and copies ran while one was open for 12% of the time, Pallas kernels for 0%

commit v1 on v0

v1 whole, which is shorter than its diff:
```python
import functools
import math

import jax
import jax.numpy as jnp
import numpy as np
from jax import lax
from jax.experimental import pallas as pl
from jax.experimental.pallas import tpu as pltpu
from jax.sharding import PartitionSpec as P

MESH = pl.DeviceIdType.MESH
f32 = jnp.float32
bf16 = jnp.bfloat16
N = 16384
W = 128


def split_np(a):
    a = np.asarray(a, np.float32)
    hi = a.astype(jnp.bfloat16)
    lo = (a - hi.astype(np.float32)).astype(jnp.bfloat16)
    return hi, lo


def tables():
    order = np.concatenate([np.arange(0, W, 2), np.arange(1, W, 2)]).astype(np.float64)
    k = np.arange(W, dtype=np.float64)
    ang = 2.0 * math.pi * (k + 0.5)[:, None] * order[None, :] / (2 * W)
    w1 = np.concatenate([np.cos(ang), -np.sin(ang)], 0)
    w1i = w1.T / N
    tw = 2.0 * math.pi * (k + 0.5)[:, None] * k[None, :] / (2 * N)
    tc, ts = np.cos(tw), np.sin(tw)
    a2 = 2.0 * math.pi * ((k[:, None] * k[None, :]) % W) / W
    c, s = np.cos(a2), np.sin(a2)
    w2 = np.block([[c, -s], [s, c]])
    return (
        *split_np(w1),
        *split_np(w2),
        *split_np(w2.T),
        *split_np(w1i),
        tc.astype(np.float32),
        ts.astype(np.float32),
    )


def split(a):
    hi = a.astype(bf16)
    lo = (a - hi.astype(f32)).astype(bf16)
    return hi, lo


def dot(a, b, dims=(((1,), (0,)), ((), ()))):
    return lax.dot_general(a, b, dims, preferred_element_type=f32)


def dot3(a, b, dims=(((1,), (0,)), ((), ()))):
    ah, al = a
    bh, bl = b
    return dot(ah, bh, dims) + (dot(al, bh, dims) + dot(ah, bl, dims))


NT = (((1,), (1,)), ((), ()))
TN = (((0,), (0,)), ((), ()))


def kernel(
    og_h, ig_h, va_h, go_h, lf_h, mf_h, *refs
):
    tab_h = refs[:10]
    go_o, gi_o, gv_o, gl_o, gm_o = refs[10:15]
    (og, ig, va, go, lf, mf) = refs[15:21]
    tab = refs[21:31]
    (send, recv, ret, back, gls, glr) = refs[31:37]
    (in_sem, tab_sem, s1, r1, s2, r2, s3, r3, ready) = refs[37:]

    me = lax.axis_index("ctx")
    z = lax.axis_index("ch")
    l = me // 2
    core = me % 2
    zo = l // 4
    bar = pltpu.get_barrier_semaphore()

    def signal(sem, ctx, ch):
        pl.semaphore_signal(sem, inc=1, device_id=(ctx, ch), device_id_type=MESH)

    ins = [
        pltpu.make_async_copy(a, b, in_sem.at[i])
        for i, (a, b) in enumerate(
            [(ig_h, ig), (va_h, va), (go_h, go), (og_h, og), (lf_h, lf), (mf_h, mf)]
        )
    ]
    for c in ins:
        c.start()
    tabs = [pltpu.make_async_copy(a, b, tab_sem.at[i]) for i, (a, b) in enumerate(zip(tab_h, tab))]

    @pl.when(core == 1)
    def _():
        def body(i, carry):
            signal(bar, lax.rem(me + i, 64), z)
            return carry

        lax.fori_loop(1, 64, body, 0)

        @pl.when(z != zo)
        def _():
            signal(bar, me, zo)

        for c in tabs:
            c.start()

    for c in ins:
        c.wait()

    product = ig[...].astype(f32) * va[...].astype(f32)
    conv = go[...].astype(f32) * og[...].astype(f32)
    filt = lf[...]
    for r, x in enumerate((product, conv, filt, filt)):
        send[pl.ds(2 * r, 32, stride=8), :] = x[:, :W]
        send[pl.ds(2 * r + 1, 32, stride=8), :] = x[:, W:]

    @pl.when(core == 0)
    def _():
        pl.semaphore_wait(bar, 32)

    @pl.when(jnp.logical_and(core == 1, z != zo))
    def _():
        pl.semaphore_wait(bar, 31)

    @pl.when(jnp.logical_and(core == 1, z == zo))
    def _():
        pl.semaphore_wait(bar, 31 + 7)

    def tile(ref, i):
        return ref.at[pl.ds(pl.multiple_of(i * 8, 8), 8)]

    def out1(i, carry):
        chip = lax.rem(l + i, 32)
        pltpu.make_async_remote_copy(
            src_ref=tile(send, chip),
            dst_ref=tile(recv, me),
            send_sem=s1,
            recv_sem=r1,
            device_id=(2 * chip + 1, z),
            device_id_type=MESH,
        ).start()
        return carry

    lax.fori_loop(1, 32, out1, 0)

    @pl.when(core == 0)
    def _():
        out1(0, 0)

    @pl.when(core == 1)
    def _():
        pltpu.make_async_copy(tile(send, l), tile(recv, me), r1).start()
        for c in tabs:
            c.wait()
        (w1h, w1l, w2h, w2l, w3h, w3l, w4h, w4l, tcr, tsr) = tab
        w1 = (w1h[...], w1l[...])
        w2 = (w2h[...], w2l[...])
        w3 = (w3h[...], w3l[...])
        w4 = (w4h[...], w4l[...])
        tc, ts = tcr[...], tsr[...]
        row = lax.broadcasted_iota(jnp.int32, (W, W), 0)
        col = lax.broadcasted_iota(jnp.int32, (W, W), 1)
        upper = col >= row
        k = jnp.broadcast_to(mf[pl.ds(l, 1), :], (W, W))
        rolled = pltpu.roll(k, 0, 1, stride=1, stride_axis=0)
        kk = jnp.concatenate([jnp.where(upper, rolled, 0.0), jnp.where(upper, 0.0, rolled)], 1)
        kk = split(kk)

        pltpu.make_async_copy(recv, recv, r1).wait()

        @pl.when(z == zo)
        def _():
            for i in range(1, 8):
                signal(ready, me, lax.rem(z + i, 8))

        def field(r):
            return recv[pl.ds(r, 64, stride=8), :]

        half_row = lax.broadcasted_iota(jnp.int32, (64, W), 0)
        pe, po = field(0), field(1)
        po_prev = jnp.where(half_row == 0, 0.0, pltpu.roll(po, 1, 0))
        pp = jnp.concatenate(
            [jnp.concatenate([pe, po_prev], 1), jnp.concatenate([po, pe], 1)], 0
        )
        pp = split(pp)
        k0 = (kk[0][:, :W], kk[1][:, :W])
        k1 = (kk[0][:, W:], kk[1][:, W:])
        p0 = (pp[0][:, :W], pp[1][:, :W])
        p1 = (pp[0][:, W:], pp[1][:, W:])
        mixed = dot3(p0, k0) + dot3(p1, k1)
        conv_f = jnp.concatenate([field(2), field(3)], 0)
        filt_f = jnp.concatenate([field(4), field(5)], 0)
        x = jnp.concatenate([mixed, conv_f, filt_f], 1)
        s = dot3(w1, split(x))
        rows = []
        for i in range(3):
            re, im = s[:W, i * W : (i + 1) * W], s[W:, i * W : (i + 1) * W]
            rows.append(jnp.concatenate([re * tc + im * ts, im * tc - re * ts], 1))
        f = dot3(split(jnp.concatenate(rows, 0)), w2)
        mr, mi = f[:W, :W], f[:W, W:]
        cr, ci = f[W : 2 * W, :W], f[W : 2 * W, W:]
        hr, hi = f[2 * W :, :W], f[2 * W :, W:]
        y = jnp.concatenate(
            [
                jnp.concatenate([mr * hr - mi * hi, mr * hi + mi * hr], 1),
                jnp.concatenate([cr * hr + ci * hi, ci * hr - cr * hi], 1),
                jnp.concatenate([cr * mr + ci * mi, ci * mr - cr * mi], 1),
            ],
            0,
        )
        t = dot3(split(y), w3)
        cols = []
        for i in range(3):
            re, im = t[i * W : (i + 1) * W, :W], t[i * W : (i + 1) * W, W:]
            cols.append(jnp.concatenate([re * tc - im * ts, im * tc + re * ts], 0))
        out = dot3(w4, split(jnp.concatenate(cols, 1)))
        recon, gmix, glong = out[:, :W], out[:, W : 2 * W], out[:, 2 * W :] * (N**-0.5)

        gls[:, 0, :] = glong[:64]
        gls[:, 1, :] = glong[64:]

        ge, gd = gmix[:64], gmix[64:]
        ge_next = jnp.where(half_row == 63, 0.0, pltpu.roll(ge, 63, 0))
        nxt = jnp.concatenate([gd, ge_next], 0)
        gms = split(gmix)
        gprod = dot3(gms, k0, NT) + dot3(split(nxt), k1, NT)
        d0 = dot3(p0, gms, TN)
        d1 = dot3(p1, gms, TN)
        d = jnp.where(upper, d0, d1)
        for bit in range(7):
            moved = pltpu.roll(d, W - (1 << bit), 1)
            d = jnp.where((row >> bit) & 1 == 1, moved, d)
        gmid = jnp.sum(d, 0, keepdims=True) * (N**-0.5)

        ret[pl.ds(0, 64, stride=8), :] = recon[:64]
        ret[pl.ds(1, 64, stride=8), :] = recon[64:]
        ret[pl.ds(2, 64, stride=8), :] = gprod[:64]
        ret[pl.ds(3, 64, stride=8), :] = gprod[64:]
        for r in range(4, 8):
            ret[pl.ds(r, 64, stride=8), :] = jnp.broadcast_to(gmid, (64, W))

        def out2(i, carry):
            d = lax.rem(me + i, 64)
            pltpu.make_async_remote_copy(
                src_ref=tile(ret, d),
                dst_ref=tile(back, l),
                send_sem=s2,
                recv_sem=r2,
                device_id=(d, z),
                device_id_type=MESH,
            ).start()
            return carry

        lax.fori_loop(1, 64, out2, 0)
        pltpu.make_async_copy(tile(ret, me), tile(back, l), r2).start()

        @pl.when(z != zo)
        def _():
            pl.semaphore_wait(ready, 1)

        slot = z * 4 + l % 4

        def out3(i, carry):
            d = lax.rem(me + i, 64)
            pltpu.make_async_remote_copy(
                src_ref=gls.at[d],
                dst_ref=glr.at[slot],
                send_sem=s3,
                recv_sem=r3,
                device_id=(d, zo),
                device_id_type=MESH,
            ).start()
            return carry

        lax.fori_loop(1, 64, out3, 0)

        @pl.when(z != zo)
        def _():
            out3(0, 0)

        @pl.when(z == zo)
        def _():
            pltpu.make_async_copy(gls.at[me], glr.at[slot], r3).start()

    pltpu.make_async_copy(back, back, r2).wait()
    recon = jnp.concatenate([back[pl.ds(0, 32, stride=8), :], back[pl.ds(1, 32, stride=8), :]], 1)
    gprod = jnp.concatenate([back[pl.ds(2, 32, stride=8), :], back[pl.ds(3, 32, stride=8), :]], 1)
    go_o[...] = (go[...].astype(f32) * recon).astype(bf16)
    gi_o[...] = (gprod * va[...].astype(f32)).astype(bf16)
    gv_o[...] = (gprod * ig[...].astype(f32)).astype(bf16)
    gm_o[...] = back[pl.ds(4, 32, stride=8), :]
    pltpu.make_async_copy(glr, glr, r3).wait()
    total = glr[0:4]
    for i in range(1, 8):
        total = total + glr[4 * i : 4 * i + 4]
    gl_o[:, :W] = total[:, 0, :]
    gl_o[:, W:] = total[:, 1, :]

    def left(ref, count, sem):
        part = ref.at[pl.ds(0, count)]
        pltpu.make_async_copy(part, part, sem).wait()

    @pl.when(core == 0)
    def _():
        left(send, 32 * 8, s1)

    @pl.when(core == 1)
    def _():
        left(send, 31 * 8, s1)
        left(ret, 63 * 8, s2)

        @pl.when(z != zo)
        def _():
            left(gls, 64, s3)

        @pl.when(z == zo)
        def _():
            left(gls, 63, s3)


def local(outer_gate, inner_gate, values, grad_out, long_filter, mid_filter):
    tabs = tables()
    vm = pltpu.VMEM
    dma = pltpu.SemaphoreType.DMA
    any_spec = pl.BlockSpec(memory_space=pl.ANY)
    vmem_spec = pl.BlockSpec(memory_space=vm)
    ins = (outer_gate, inner_gate, values, grad_out, long_filter, mid_filter)
    return pl.pallas_call(
        kernel,
        out_shape=[
            jax.ShapeDtypeStruct((32, 256), bf16),
            jax.ShapeDtypeStruct((32, 256), bf16),
            jax.ShapeDtypeStruct((32, 256), bf16),
            jax.ShapeDtypeStruct((4, 256), f32),
            jax.ShapeDtypeStruct((32, W), f32),
        ],
        in_specs=[any_spec] * 16,
        out_specs=[vmem_spec] * 5,
        scratch_shapes=[
            *[vm((32, 256), bf16)] * 4,
            vm((32, 256), f32),
            vm((32, W), f32),
            *[vm(t.shape, t.dtype) for t in tabs],
            vm((32 * 8, W), f32),
            vm((64 * 8, W), f32),
            vm((64 * 8, W), f32),
            vm((32 * 8, W), f32),
            vm((64, 2, W), f32),
            vm((32, 2, W), f32),
            dma((6,)),
            dma((10,)),
            *[dma] * 6,
            pltpu.SemaphoreType.REGULAR,
        ],
        compiler_params=pltpu.CompilerParams(
            collective_id=0, has_side_effects=True, vmem_limit_bytes=32 * 1024 * 1024
        ),
    )(*ins, *[jnp.asarray(t) for t in tabs])


def solution(mesh):
    in_specs = (
        P("ch", "ctx"),
        P("ch", "ctx"),
        P("ch", "ctx"),
        P("ch", "ctx"),
        P(None, "ctx"),
        P("ch", None),
    )
    out_specs = (P("ch", "ctx"), P("ch", "ctx"), P("ch", "ctx"), P("ch", "ctx"), P("ch", None))
    return jax.shard_map(local, mesh=mesh, in_specs=in_specs, out_specs=out_specs, check_vma=False)
```

time: 574 us -> 51 us (0.09)
  the two profiles are of different devices: /device:TPU:1 before, /device:TPU:65 now
where the time goes in v1:
time: 51 us; the launch traced here: 50.2 us
  Pallas kernels  33.6 us (66%)
  local copies, waits for them, and re-layouts  16 us (31%)
  between operations  0.67 us (1%)
    pallas_call x1, Pallas kernels, local(): pl.pallas_call(kernel, out_shape=[jax.ShapeDtypeStruct((32, 256), bf16),...  33.6 us
    unnamed x37, local copies, waits for them, and re-layouts  16 us

profile of v1, /device:TPU:65, one launch (start us, length us, event | category | flops | bytes accessed | tf_op | source)
XLA Modules:
  0.0 50.2 jit_solution(3550445667720083748)
XLA Ops:
  0.6 0.0 copy-start
  0.6 0.9 %copy-done = bf16[256,256]{1,0:T(8,128)(2,1)S(1)} copy-done((bf16[256,256]{1,0:T(8,128)(2,1)S(1)}, bf16[256,256]{1,0:T(8,128)(2,1)}, u32[]{:S(2)}) %copy-start) | copy-done | bytes 131096
  1.5 0.0 copy-start.1
  1.5 0.9 %copy-done.1 = bf16[256,256]{1,0:T(8,128)(2,1)S(1)} copy-done((bf16[256,256]{1,0:T(8,128)(2,1)S(1)}, bf16[256,256]{1,0:T(8,128)(2,1)}, u32[]{:S(2)}) %copy-start.1) | copy-done | bytes 131096
  2.4 0.0 copy-start.2
  2.4 0.9 %copy-done.2 = bf16[256,256]{1,0:T(8,128)(2,1)S(1)} copy-done((bf16[256,256]{1,0:T(8,128)(2,1)S(1)}, bf16[256,256]{1,0:T(8,128)(2,1)}, u32[]{:S(2)}) %copy-start.2) | copy-done | bytes 131096
  3.4 0.0 copy-start.3
  3.4 0.9 %copy-done.3 = bf16[256,256]{1,0:T(8,128)(2,1)S(1)} copy-done((bf16[256,256]{1,0:T(8,128)(2,1)S(1)}, bf16[256,256]{1,0:T(8,128)(2,1)}, u32[]{:S(2)}) %copy-start.3) | copy-done | bytes 131096
  4.3 0.0 copy-start.4
  4.3 0.8 %copy-done.4 = f32[128,128]{1,0:T(8,128)S(1)} copy-done((f32[128,128]{1,0:T(8,128)S(1)}, f32[128,128]{1,0:T(8,128)}, u32[]{:S(2)}) %copy-start.4) | copy-done | bytes 65560
  5.1 0.0 copy-start.5
  5.1 0.8 %copy-done.5 = f32[128,128]{1,0:T(8,128)S(1)} copy-done((f32[128,128]{1,0:T(8,128)S(1)}, f32[128,128]{1,0:T(8,128)}, u32[]{:S(2)}) %copy-start.5) | copy-done | bytes 65560
  5.9 0.0 copy-start.6
  5.9 0.8 %copy-done.6 = bf16[128,256]{1,0:T(8,128)(2,1)S(1)} copy-done((bf16[128,256]{1,0:T(8,128)(2,1)S(1)}, bf16[128,256]{1,0:T(8,128)(2,1)}, u32[]{:S(2)}) %copy-start.6) | copy-done | bytes 65560
  6.8 0.0 copy-start.7
  6.8 0.8 %copy-done.7 = bf16[128,256]{1,0:T(8,128)(2,1)S(1)} copy-done((bf16[128,256]{1,0:T(8,128)(2,1)S(1)}, bf16[128,256]{1,0:T(8,128)(2,1)}, u32[]{:S(2)}) %copy-start.7) | copy-done | bytes 65560
  7.6 0.0 copy-start.8
  7.6 0.8 %copy-done.8 = bf16[256,128]{1,0:T(8,128)(2,1)S(1)} copy-done((bf16[256,128]{1,0:T(8,128)(2,1)S(1)}, bf16[256,128]{1,0:T(8,128)(2,1)}, u32[]{:S(2)}) %copy-start.8) | copy-done | bytes 65560
  8.5 0.0 copy-start.9
  8.5 0.8 %copy-done.9 = bf16[256,128]{1,0:T(8,128)(2,1)S(1)} copy-done((bf16[256,128]{1,0:T(8,128)(2,1)S(1)}, bf16[256,128]{1,0:T(8,128)(2,1)}, u32[]{:S(2)}) %copy-start.9) | copy-done | bytes 65560
  9.3 0.0 copy-start.10
  9.3 0.8 %copy-done.10 = f32[32,256]{1,0:T(8,128)S(1)} copy-done((f32[32,256]{1,0:T(8,128)S(1)}, f32[32,256]{1,0:T(8,128)}, u32[]{:S(2)}) %copy-start.10) | copy-done | bytes 32792
  10.1 0.0 copy-start.11
  10.1 0.7 %copy-done.11 = bf16[32,256]{1,0:T(8,128)(2,1)S(1)} copy-done((bf16[32,256]{1,0:T(8,128)(2,1)S(1)}, bf16[32,256]{1,0:T(8,128)(2,1)}, u32[]{:S(2)}) %copy-start.11) | copy-done | bytes 16408
  10.8 0.0 copy-start.12
  10.8 0.7 %copy-done.12 = bf16[32,256]{1,0:T(8,128)(2,1)S(1)} copy-done((bf16[32,256]{1,0:T(8,128)(2,1)S(1)}, bf16[32,256]{1,0:T(8,128)(2,1)}, u32[]{:S(2)}) %copy-start.12) | copy-done | bytes 16408
  11.5 0.0 copy-start.13
  11.5 0.7 %copy-done.13 = bf16[32,256]{1,0:T(8,128)(2,1)S(1)} copy-done((bf16[32,256]{1,0:T(8,128)(2,1)S(1)}, bf16[32,256]{1,0:T(8,128)(2,1)}, u32[]{:S(2)}) %copy-start.13) | copy-done | bytes 16408
  12.2 0.0 copy-start.14
  12.2 0.7 %copy-done.14 = bf16[32,256]{1,0:T(8,128)(2,1)S(1)} copy-done((bf16[32,256]{1,0:T(8,128)(2,1)S(1)}, bf16[32,256]{1,0:T(8,128)(2,1)}, u32[]{:S(2)}) %copy-start.14) | copy-done | bytes 16408
  12.9 0.0 copy-start.15
  12.9 0.7 %copy-done.15 = f32[32,128]{1,0:T(8,128)S(1)} copy-done((f32[32,128]{1,0:T(8,128)S(1)}, f32[32,128]{1,0:T(8,128)}, u32[]{:S(2)}) %copy-start.15) | copy-done | bytes 16408
  13.6 33.6 %shard_map.191 = (bf16[32,256]{1,0:T(8,128)(2,1)S(1)}, bf16[32,256]{1,0:T(8,128)(2,1)S(1)}, bf16[32,256]{1,0:T(8,128)(2,1)S(1)}, f32[4,256]{1,0:T(4,128)S(1)}, f32[32,128]{1,0:T(8,128)S(1)}) custom-call(bf16[32,256]{1,0:T(8,128)(2,1)S(1)} %copy-done.11, bf16[32,256]{1,0:T(8,128)(2,1)S(1)} %copy-done.12, bf16[32,256]{1,0:T(8,128)(2,1)S(1)} %copy-done.13, ...), custom_call_target="tpu_custom_call" | custom-call | tf_op jit(solution)/shard_map/pallas_call | solution.py:333
  47.2 0.6 %copy.26 = bf16[32,256]{1,0:T(8,128)(2,1)} copy(bf16[32,256]{1,0:T(8,128)(2,1)S(1)} %get-tuple-element.10) | data formatting | bytes 32768
  47.8 0.6 %copy.27 = bf16[32,256]{1,0:T(8,128)(2,1)} copy(bf16[32,256]{1,0:T(8,128)(2,1)S(1)} %get-tuple-element.11) | data formatting | bytes 32768
  48.4 0.6 %copy.28 = bf16[32,256]{1,0:T(8,128)(2,1)} copy(bf16[32,256]{1,0:T(8,128)(2,1)S(1)} %get-tuple-element.12) | data formatting | bytes 32768
  49.0 0.6 %copy.29 = f32[4,256]{1,0:T(4,128)} copy(f32[4,256]{1,0:T(4,128)S(1)} %get-tuple-element.13) | data formatting | bytes 8192
  49.6 0.6 %copy.30 = f32[32,128]{1,0:T(8,128)} copy(f32[32,128]{1,0:T(8,128)S(1)} %get-tuple-element.14) | data formatting | bytes 32768
Async XLA Ops:
  0.6 0.9 %copy-start = (bf16[256,256]{1,0:T(8,128)(2,1)S(1)}, bf16[256,256]{1,0:T(8,128)(2,1)}, u32[]{:S(2)}) copy-start(bf16[256,256]{1,0:T(8,128)(2,1)} %constant.25.clone.refs_5_) | copy-start | bytes 393220
  1.5 0.9 %copy-start.1 = (bf16[256,256]{1,0:T(8,128)(2,1)S(1)}, bf16[256,256]{1,0:T(8,128)(2,1)}, u32[]{:S(2)}) copy-start(bf16[256,256]{1,0:T(8,128)(2,1)} %constant.24.clone.refs_4_) | copy-start | bytes 393220
  2.4 0.9 %copy-start.2 = (bf16[256,256]{1,0:T(8,128)(2,1)S(1)}, bf16[256,256]{1,0:T(8,128)(2,1)}, u32[]{:S(2)}) copy-start(bf16[256,256]{1,0:T(8,128)(2,1)} %constant.23.clone.refs_3_) | copy-start | bytes 393220
  3.4 0.9 %copy-start.3 = (bf16[256,256]{1,0:T(8,128)(2,1)S(1)}, bf16[256,256]{1,0:T(8,128)(2,1)}, u32[]{:S(2)}) copy-start(bf16[256,256]{1,0:T(8,128)(2,1)} %constant.22.clone.refs_2_) | copy-start | bytes 393220
  4.3 0.8 %copy-start.4 = (f32[128,128]{1,0:T(8,128)S(1)}, f32[128,128]{1,0:T(8,128)}, u32[]{:S(2)}) copy-start(f32[128,128]{1,0:T(8,128)} %constant.29.clone.refs_9_) | copy-start | bytes 196612
  5.1 0.8 %copy-start.5 = (f32[128,128]{1,0:T(8,128)S(1)}, f32[128,128]{1,0:T(8,128)}, u32[]{:S(2)}) copy-start(f32[128,128]{1,0:T(8,128)} %constant.28.clone.refs_8_) | copy-start | bytes 196612
  5.9 0.8 %copy-start.6 = (bf16[128,256]{1,0:T(8,128)(2,1)S(1)}, bf16[128,256]{1,0:T(8,128)(2,1)}, u32[]{:S(2)}) copy-start(bf16[128,256]{1,0:T(8,128)(2,1)} %constant.27.clone.refs_7_) | copy-start | bytes 196612
  6.8 0.8 %copy-start.7 = (bf16[128,256]{1,0:T(8,128)(2,1)S(1)}, bf16[128,256]{1,0:T(8,128)(2,1)}, u32[]{:S(2)}) copy-start(bf16[128,256]{1,0:T(8,128)(2,1)} %constant.26.clone.refs_6_) | copy-start | bytes 196612
  7.6 0.8 %copy-start.8 = (bf16[256,128]{1,0:T(8,128)(2,1)S(1)}, bf16[256,128]{1,0:T(8,128)(2,1)}, u32[]{:S(2)}) copy-start(bf16[256,128]{1,0:T(8,128)(2,1)} %constant.21.clone.refs_1_) | copy-start | bytes 196612
  8.5 0.8 %copy-start.9 = (bf16[256,128]{1,0:T(8,128)(2,1)S(1)}, bf16[256,128]{1,0:T(8,128)(2,1)}, u32[]{:S(2)}) copy-start(bf16[256,128]{1,0:T(8,128)(2,1)} %constant.20.clone.refs_0_) | copy-start | bytes 196612
  9.3 0.8 %copy-start.10 = (f32[32,256]{1,0:T(8,128)S(1)}, f32[32,256]{1,0:T(8,128)}, u32[]{:S(2)}) copy-start(f32[32,256]{1,0:T(8,128)} %lf_h.1) | copy-start | bytes 98308
  10.1 0.7 %copy-start.11 = (bf16[32,256]{1,0:T(8,128)(2,1)S(1)}, bf16[32,256]{1,0:T(8,128)(2,1)}, u32[]{:S(2)}) copy-start(bf16[32,256]{1,0:T(8,128)(2,1)} %og_h.1) | copy-start | bytes 49156
  10.8 0.7 %copy-start.12 = (bf16[32,256]{1,0:T(8,128)(2,1)S(1)}, bf16[32,256]{1,0:T(8,128)(2,1)}, u32[]{:S(2)}) copy-start(bf16[32,256]{1,0:T(8,128)(2,1)} %ig_h.1) | copy-start | bytes 49156
  11.5 0.7 %copy-start.13 = (bf16[32,256]{1,0:T(8,128)(2,1)S(1)}, bf16[32,256]{1,0:T(8,128)(2,1)}, u32[]{:S(2)}) copy-start(bf16[32,256]{1,0:T(8,128)(2,1)} %va_h.1) | copy-start | bytes 49156
  12.2 0.7 %copy-start.14 = (bf16[32,256]{1,0:T(8,128)(2,1)S(1)}, bf16[32,256]{1,0:T(8,128)(2,1)}, u32[]{:S(2)}) copy-start(bf16[32,256]{1,0:T(8,128)(2,1)} %go_h.1) | copy-start | bytes 49156
  12.9 0.7 %copy-start.15 = (f32[32,128]{1,0:T(8,128)S(1)}, f32[32,128]{1,0:T(8,128)}, u32[]{:S(2)}) copy-start(f32[32,128]{1,0:T(8,128)} %mf_h.1) | copy-start | bytes 49156

commit v2 on v1

v2 whole, which is shorter than its diff:
```python
import functools
import math

import jax
import jax.numpy as jnp
import numpy as np
from jax import lax
from jax.experimental import pallas as pl
from jax.experimental.pallas import tpu as pltpu
from jax.sharding import PartitionSpec as P

MESH = pl.DeviceIdType.MESH
f32 = jnp.float32
bf16 = jnp.bfloat16
N = 16384
W = 128


def split_np(a):
    a = np.asarray(a, np.float32)
    hi = a.astype(jnp.bfloat16)
    lo = (a - hi.astype(np.float32)).astype(jnp.bfloat16)
    return hi, lo


def tables():
    order = np.concatenate([np.arange(0, W, 2), np.arange(1, W, 2)]).astype(np.float64)
    k = np.arange(W, dtype=np.float64)
    ang = 2.0 * math.pi * (k + 0.5)[:, None] * order[None, :] / (2 * W)
    w1 = np.concatenate([np.cos(ang), -np.sin(ang)], 0)
    w1i = w1.T / N
    tw = 2.0 * math.pi * (k + 0.5)[:, None] * k[None, :] / (2 * N)
    tc, ts = np.cos(tw), np.sin(tw)
    a2 = 2.0 * math.pi * ((k[:, None] * k[None, :]) % W) / W
    c, s = np.cos(a2), np.sin(a2)
    w2 = np.block([[c, -s], [s, c]])
    return (
        *split_np(w1),
        *split_np(w2),
        *split_np(w2.T),
        *split_np(w1i),
        tc.astype(np.float32),
        ts.astype(np.float32),
    )


def split(a):
    hi = a.astype(bf16)
    lo = (a - hi.astype(f32)).astype(bf16)
    return hi, lo


def dot(a, b, dims=(((1,), (0,)), ((), ()))):
    return lax.dot_general(a, b, dims, preferred_element_type=f32)


def dot3(a, b, dims=(((1,), (0,)), ((), ()))):
    ah, al = a
    bh, bl = b
    return dot(ah, bh, dims) + (dot(al, bh, dims) + dot(ah, bl, dims))


NT = (((1,), (1,)), ((), ()))
TN = (((0,), (0,)), ((), ()))


def ring(d, n):
    return min(d, n - d)


OFFSETS = sorted(
    [(dx, dy) for dx in range(4) for dy in range(8)], key=lambda o: -(ring(o[0], 4) + ring(o[1], 8))
)


def kernel(og_h, ig_h, va_h, go_h, lf_h, mf_h, *refs):
    tab_h = refs[:10]
    outs_h = refs[10:14]
    glr = refs[14]
    (og, ig, va, go, lf, mf) = refs[15:21]
    tab = refs[21:31]
    outs = refs[31:35]
    go_o, gi_o, gv_o, gm_o = outs
    (send, recv, ret, back, gls) = refs[35:40]
    (in_sem, tab_sem, out_sem, s1, r1, s2, r2, s3, r3, ready) = refs[40:]

    me = lax.axis_index("ctx")
    z = lax.axis_index("ch")
    l = me // 2
    px, py = l // 8, l % 8
    works = me % 2 == 1
    zo = l // 4
    hub = z == zo
    bar = pltpu.get_barrier_semaphore()

    def signal(sem, ctx, ch):
        pl.semaphore_signal(sem, inc=1, device_id=(ctx, ch), device_id_type=MESH)

    def chip_at(dx, dy):
        return lax.rem(px + dx, 4) * 8 + lax.rem(py + dy, 8)

    ins = [
        pltpu.make_async_copy(a, b, in_sem.at[i])
        for i, (a, b) in enumerate(
            [(ig_h, ig), (va_h, va), (go_h, go), (og_h, og), (lf_h, lf), (mf_h, mf)]
        )
    ]
    for c in ins:
        c.start()
    tabs = [pltpu.make_async_copy(a, b, tab_sem.at[i]) for i, (a, b) in enumerate(zip(tab_h, tab))]

    @pl.when(works)
    def _():
        for dx, dy in OFFSETS:
            chip = chip_at(dx, dy)
            signal(bar, 2 * chip, z)
            if (dx, dy) != (0, 0):
                signal(bar, 2 * chip + 1, z)

        @pl.when(jnp.logical_not(hub))
        def _():
            signal(bar, me, zo)

        for c in tabs:
            c.start()

    for c in ins:
        c.wait()

    product = ig[...].astype(f32) * va[...].astype(f32)
    conv = go[...].astype(f32) * og[...].astype(f32)
    filt = lf[...]
    for r, x in enumerate((product, conv, filt, filt)):
        send[pl.ds(2 * r, 32, stride=8), :] = x[:, :W]
        send[pl.ds(2 * r + 1, 32, stride=8), :] = x[:, W:]

    @pl.when(jnp.logical_not(works))
    def _():
        pl.semaphore_wait(bar, 32)

    @pl.when(jnp.logical_and(works, jnp.logical_not(hub)))
    def _():
        pl.semaphore_wait(bar, 31)

    @pl.when(jnp.logical_and(works, hub))
    def _():
        pl.semaphore_wait(bar, 38)

    def tile(ref, i):
        return ref.at[pl.ds(pl.multiple_of(i * 8, 8), 8)]

    def out1(chip):
        pltpu.make_async_remote_copy(
            src_ref=tile(send, chip),
            dst_ref=tile(recv, me),
            send_sem=s1,
            recv_sem=r1,
            device_id=(2 * chip + 1, z),
            device_id_type=MESH,
        ).start()

    for dx, dy in OFFSETS[:-1]:
        out1(chip_at(dx, dy))

    @pl.when(jnp.logical_not(works))
    def _():
        out1(l)

    @pl.when(works)
    def _():
        pltpu.make_async_copy(tile(send, l), tile(recv, me), r1).start()
        for c in tabs:
            c.wait()
        (w1h, w1l, w2h, w2l, w3h, w3l, w4h, w4l, tcr, tsr) = tab
        w1 = (w1h[...], w1l[...])
        w2 = (w2h[...], w2l[...])
        w3 = (w3h[...], w3l[...])
        w4 = (w4h[...], w4l[...])
        tc, ts = tcr[...], tsr[...]
        row = lax.broadcasted_iota(jnp.int32, (W, W), 0)
        col = lax.broadcasted_iota(jnp.int32, (W, W), 1)
        upper = col >= row
        half_row = lax.broadcasted_iota(jnp.int32, (64, W), 0)
        k = jnp.broadcast_to(mf[pl.ds(l, 1), :], (W, W))
        rolled = pltpu.roll(k, 0, 1, stride=1, stride_axis=0)
        k0 = split(jnp.where(upper, rolled, 0.0))
        k1 = split(jnp.where(upper, 0.0, rolled))

        pltpu.make_async_copy(recv, recv, r1).wait()

        @pl.when(hub)
        def _():
            for i in (4, 3, 5, 2, 6, 1, 7):
                signal(ready, me, lax.rem(z + i, 8))

        def field(r):
            return recv[pl.ds(r, 64, stride=8), :]

        def both(r):
            return jnp.concatenate([field(r), field(r + 1)], 0)

        def forward(x):
            s = dot3(w1, split(x))
            parts = []
            for i in range(x.shape[1] // W):
                re, im = s[:W, i * W : (i + 1) * W], s[W:, i * W : (i + 1) * W]
                parts.append(jnp.concatenate([re * tc + im * ts, im * tc - re * ts], 1))
            return dot3(split(jnp.concatenate(parts, 0)), w2)

        def inverse(y):
            t = dot3(split(y), w3)
            parts = []
            for i in range(y.shape[0] // W):
                re, im = t[i * W : (i + 1) * W, :W], t[i * W : (i + 1) * W, W:]
                parts.append(jnp.concatenate([re * tc - im * ts, im * tc + re * ts], 0))
            return dot3(w4, split(jnp.concatenate(parts, 1)))

        pe, po = field(0), field(1)
        po_prev = jnp.where(half_row == 0, 0.0, pltpu.roll(po, 1, 0))
        p0 = split(jnp.concatenate([pe, po], 0))
        p1 = split(jnp.concatenate([po_prev, pe], 0))
        mixed = dot3(p0, k0) + dot3(p1, k1)
        f = forward(jnp.concatenate([mixed, both(2)], 1))
        mr, mi = f[:W, :W], f[:W, W:]
        cr, ci = f[W:, :W], f[W:, W:]
        glong = inverse(jnp.concatenate([cr * mr + ci * mi, ci * mr - cr * mi], 1)) * (N**-0.5)
        gls[:, 0, :] = glong[:64]
        gls[:, 1, :] = glong[64:]

        @pl.when(jnp.logical_not(hub))
        def _():
            pl.semaphore_wait(ready, 1)

        slot = z * 4 + l % 4

        def out3(d):
            pltpu.make_async_remote_copy(
                src_ref=gls.at[d],
                dst_ref=glr.at[slot],
                send_sem=s3,
                recv_sem=r3,
                device_id=(d, zo),
                device_id_type=MESH,
            ).start()

        for dx, dy in OFFSETS:
            chip = chip_at(dx, dy)
            out3(2 * chip)
            if (dx, dy) != (0, 0):
                out3(2 * chip + 1)

        @pl.when(jnp.logical_not(hub))
        def _():
            out3(me)

        @pl.when(hub)
        def _():
            pltpu.make_async_copy(gls.at[me], glr.at[slot], r3).start()

        h = forward(both(4))
        hr, hi = h[:, :W], h[:, W:]
        out = inverse(
            jnp.concatenate(
                [
                    jnp.concatenate([mr * hr - mi * hi, mr * hi + mi * hr], 1),
                    jnp.concatenate([cr * hr + ci * hi, ci * hr - cr * hi], 1),
                ],
                0,
            )
        )
        recon, gmix = out[:, :W], out[:, W:]
        ge, gd = gmix[:64], gmix[64:]
        ge_next = jnp.where(half_row == 63, 0.0, pltpu.roll(ge, 63, 0))
        gms = split(gmix)
        gprod = dot3(gms, k0, NT) + dot3(split(jnp.concatenate([gd, ge_next], 0)), k1, NT)
        d = jnp.where(upper, dot3(p0, gms, TN), dot3(p1, gms, TN))
        for bit in range(7):
            moved = pltpu.roll(d, W - (1 << bit), 1)
            d = jnp.where((row >> bit) & 1 == 1, moved, d)
        gmid = jnp.sum(d, 0, keepdims=True) * (N**-0.5)

        ret[pl.ds(0, 64, stride=8), :] = recon[:64]
        ret[pl.ds(1, 64, stride=8), :] = recon[64:]
        ret[pl.ds(2, 64, stride=8), :] = gprod[:64]
        ret[pl.ds(3, 64, stride=8), :] = gprod[64:]
        for r in range(4, 8):
            ret[pl.ds(r, 64, stride=8), :] = jnp.broadcast_to(gmid, (64, W))

        def out2(d):
            pltpu.make_async_remote_copy(
                src_ref=tile(ret, d),
                dst_ref=tile(back, l),
                send_sem=s2,
                recv_sem=r2,
                device_id=(d, z),
                device_id_type=MESH,
            ).start()

        for dx, dy in OFFSETS:
            chip = chip_at(dx, dy)
            out2(2 * chip)
            if (dx, dy) != (0, 0):
                out2(2 * chip + 1)
        pltpu.make_async_copy(tile(ret, me), tile(back, l), r2).start()

    def left(ref, count, sem):
        part = ref.at[pl.ds(0, count)]
        pltpu.make_async_copy(part, part, sem).wait()

    left(send, 31 * 8, s1)

    @pl.when(jnp.logical_not(works))
    def _():
        left(send, 8, s1)

    @pl.when(works)
    def _():
        left(gls, 63, s3)
        left(ret, 63 * 8, s2)

        @pl.when(jnp.logical_not(hub))
        def _():
            left(gls, 1, s3)

    pltpu.make_async_copy(back, back, r2).wait()

    def rows(r):
        return back[pl.ds(r, 32, stride=8), :]

    recon = jnp.concatenate([rows(0), rows(1)], 1)
    gprod = jnp.concatenate([rows(2), rows(3)], 1)
    go_o[...] = (go[...].astype(f32) * recon).astype(bf16)
    gi_o[...] = (gprod * va[...].astype(f32)).astype(bf16)
    gv_o[...] = (gprod * ig[...].astype(f32)).astype(bf16)
    gm_o[...] = rows(4)
    leave = [pltpu.make_async_copy(a, b, out_sem.at[i]) for i, (a, b) in enumerate(zip(outs, outs_h))]
    for c in leave:
        c.start()
    for c in leave:
        c.wait()
    pltpu.make_async_copy(glr, glr, r3).wait()


def deliver(a, b, c, m, parts, a_o, b_o, c_o, gl_o, m_o):
    a_o[...] = a[...]
    b_o[...] = b[...]
    c_o[...] = c[...]
    m_o[...] = m[...]
    total = parts[0:4]
    for i in range(1, 8):
        total = total + parts[4 * i : 4 * i + 4]
    gl_o[:, :W] = total[:, 0, :]
    gl_o[:, W:] = total[:, 1, :]


def local(outer_gate, inner_gate, values, grad_out, long_filter, mid_filter):
    tabs = tables()
    vm = pltpu.VMEM
    dma = pltpu.SemaphoreType.DMA
    hbm = pl.BlockSpec(memory_space=pl.ANY)
    vmem = pl.BlockSpec(memory_space=vm)
    ins = (outer_gate, inner_gate, values, grad_out, long_filter, mid_filter)
    outs = [((32, 256), bf16)] * 3 + [((32, W), f32)]
    shapes = [jax.ShapeDtypeStruct(*o) for o in outs]
    results = pl.pallas_call(
        kernel,
        out_shape=[*shapes, jax.ShapeDtypeStruct((32, 2, W), f32)],
        in_specs=[hbm] * 16,
        out_specs=[hbm] * 5,
        scratch_shapes=[
            *[vm((32, 256), bf16)] * 4,
            vm((32, 256), f32),
            vm((32, W), f32),
            *[vm(t.shape, t.dtype) for t in tabs],
            *[vm(*o) for o in outs],
            vm((32 * 8, W), f32),
            vm((64 * 8, W), f32),
            vm((64 * 8, W), f32),
            vm((32 * 8, W), f32),
            vm((64, 2, W), f32),
            dma((6,)),
            dma((10,)),
            dma((4,)),
            *[dma] * 6,
            pltpu.SemaphoreType.REGULAR,
        ],
        compiler_params=pltpu.CompilerParams(collective_id=0, has_side_effects=True),
    )(*ins, *[jnp.asarray(t) for t in tabs])
    return pl.pallas_call(
        deliver,
        out_shape=[*shapes[:3], jax.ShapeDtypeStruct((4, 256), f32), shapes[3]],
        in_specs=[vmem] * 5,
        out_specs=[vmem] * 5,
    )(*results)


def solution(mesh):
    in_specs = (
        P("ch", "ctx"),
        P("ch", "ctx"),
        P("ch", "ctx"),
        P("ch", "ctx"),
        P(None, "ctx"),
        P("ch", None),
    )
    out_specs = (P("ch", "ctx"), P("ch", "ctx"), P("ch", "ctx"), P("ch", "ctx"), P("ch", None))
    return jax.shard_map(local, mesh=mesh, in_specs=in_specs, out_specs=out_specs, check_vma=False)
```

time: 51 us -> 36.1 us (0.71)
  the two profiles are of different devices: /device:TPU:65 before, /device:TPU:1 now
where the time goes in v2:
time: 36.1 us; the launch traced here: 35.8 us
  Pallas kernels  35.1 us (97%)
  between operations  0.64 us (2%)
    pallas_call x1, Pallas kernels, local(): pl.pallas_call(kernel, out_shape=[*shapes, jax.ShapeDtypeStruct((32, 2, W...  33.7 us
    pallas_call x1, Pallas kernels, local(): pl.pallas_call(deliver, out_shape=[*shapes[:3], jax.ShapeDtypeStruct((4,...  1.46 us

profile of v2, /device:TPU:1, one launch (start us, length us, event | category | flops | bytes accessed | tf_op | source)
XLA Modules:
  0.0 35.8 jit_solution(2945822117432551650)
XLA Ops:
  0.6 33.7 %shard_map.191 = (bf16[32,256]{1,0:T(8,128)(2,1)}, bf16[32,256]{1,0:T(8,128)(2,1)}, bf16[32,256]{1,0:T(8,128)(2,1)}, f32[32,128]{1,0:T(8,128)}, f32[32,2,128]{2,1,0:T(2,128)}) custom-call(bf16[32,256]{1,0:T(8,128)(2,1)} %og_h.1, bf16[32,256]{1,0:T(8,128)(2,1)} %ig_h.1, bf16[32,256]{1,0:T(8,128)(2,1)} %va_h.1, bf16[32,256]{1,0:T(8,128)(2,1)} %go_h.1, ...), custom_call_target="tpu_custom_call" | custom-call | tf_op jit(solution)/shard_map/pallas_call | solution.py:365
  34.3 1.5 %shard_map.192 = (bf16[32,256]{1,0:T(8,128)(2,1)}, bf16[32,256]{1,0:T(8,128)(2,1)}, bf16[32,256]{1,0:T(8,128)(2,1)}, f32[4,256]{1,0:T(4,128)}, f32[32,128]{1,0:T(8,128)}) custom-call(bf16[32,256]{1,0:T(8,128)(2,1)} %get-tuple-element.10.a, bf16[32,256]{1,0:T(8,128)(2,1)} %get-tuple-element.11.b, bf16[32,256]{1,0:T(8,128)(2,1)} %get-tuple-element.12.c, ...), custom_call_target="tpu_custom_call" | custom-call | tf_op jit(solution)/shard_map/pallas_call | solution.py:389

commit v3 on v2

--- a/solution.py
+++ b/solution.py
@@ -81,8 +81,8 @@
     tab = refs[21:31]
     outs = refs[31:35]
     go_o, gi_o, gv_o, gm_o = outs
-    (send, recv, ret, back, gls) = refs[35:40]
-    (in_sem, tab_sem, out_sem, s1, r1, s2, r2, s3, r3, ready) = refs[40:]
+    (send, recv, send_f, recv_f, ret, back, gls) = refs[35:42]
+    (in_sem, tab_sem, out_sem, s1, r1, s2, r2, s3, r3, s4, r4, ready) = refs[42:]
 
     me = lax.axis_index("ctx")
     z = lax.axis_index("ch")
@@ -130,9 +130,12 @@
     product = ig[...].astype(f32) * va[...].astype(f32)
     conv = go[...].astype(f32) * og[...].astype(f32)
     filt = lf[...]
-    for r, x in enumerate((product, conv, filt, filt)):
-        send[pl.ds(2 * r, 32, stride=8), :] = x[:, :W]
-        send[pl.ds(2 * r + 1, 32, stride=8), :] = x[:, W:]
+    send[:, 0, :] = product[:, :W]
+    send[:, 1, :] = product[:, W:]
+    send[:, 2, :] = conv[:, :W]
+    send[:, 3, :] = conv[:, W:]
+    send_f[:, 0, :] = filt[:, :W]
+    send_f[:, 1, :] = filt[:, W:]
 
     @pl.when(jnp.logical_not(works))
     def _():
@@ -149,26 +152,35 @@
     def tile(ref, i):
         return ref.at[pl.ds(pl.multiple_of(i * 8, 8), 8)]
 
-    def out1(chip):
+    def out(src, dst, ssem, rsem, d, p):
         pltpu.make_async_remote_copy(
-            src_ref=tile(send, chip),
-            dst_ref=tile(recv, me),
-            send_sem=s1,
-            recv_sem=r1,
-            device_id=(2 * chip + 1, z),
+            src_ref=src,
+            dst_ref=dst,
+            send_sem=ssem,
+            recv_sem=rsem,
+            device_id=(d, p),
             device_id_type=MESH,
         ).start()
 
-    for dx, dy in OFFSETS[:-1]:
-        out1(chip_at(dx, dy))
+    def out_tokens(chip):
+        out(send.at[chip], recv.at[me], s1, r1, 2 * chip + 1, z)
+
+    def out_filter(chip):
+        out(send_f.at[chip], recv_f.at[me], s4, r4, 2 * chip + 1, z)
+
+    for put in (out_tokens, out_filter):
+        for dx, dy in OFFSETS[:-1]:
+            put(chip_at(dx, dy))
 
     @pl.when(jnp.logical_not(works))
     def _():
-        out1(l)
+        out_tokens(l)
+        out_filter(l)
 
     @pl.when(works)
     def _():
-        pltpu.make_async_copy(tile(send, l), tile(recv, me), r1).start()
+        pltpu.make_async_copy(send.at[l], recv.at[me], r1).start()
+        pltpu.make_async_copy(send_f.at[l], recv_f.at[me], r4).start()
         for c in tabs:
             c.wait()
         (w1h, w1l, w2h, w2l, w3h, w3l, w4h, w4l, tcr, tsr) = tab
@@ -193,12 +205,6 @@
             for i in (4, 3, 5, 2, 6, 1, 7):
                 signal(ready, me, lax.rem(z + i, 8))
 
-        def field(r):
-            return recv[pl.ds(r, 64, stride=8), :]
-
-        def both(r):
-            return jnp.concatenate([field(r), field(r + 1)], 0)
-
         def forward(x):
             s = dot3(w1, split(x))
             parts = []
@@ -215,51 +221,48 @@
                 parts.append(jnp.concatenate([re * tc - im * ts, im * tc + re * ts], 0))
             return dot3(w4, split(jnp.concatenate(parts, 1)))
 
-        pe, po = field(0), field(1)
+        pe, po = recv[:, 0, :], recv[:, 1, :]
         po_prev = jnp.where(half_row == 0, 0.0, pltpu.roll(po, 1, 0))
         p0 = split(jnp.concatenate([pe, po], 0))
         p1 = split(jnp.concatenate([po_prev, pe], 0))
         mixed = dot3(p0, k0) + dot3(p1, k1)
-        f = forward(jnp.concatenate([mixed, both(2)], 1))
+        conv_f = jnp.concatenate([recv[:, 2, :], recv[:, 3, :]], 0)
+        f = forward(jnp.concatenate([mixed, conv_f], 1))
         mr, mi = f[:W, :W], f[:W, W:]
         cr, ci = f[W:, :W], f[W:, W:]
         glong = inverse(jnp.concatenate([cr * mr + ci * mi, ci * mr - cr * mi], 1)) * (N**-0.5)
         gls[:, 0, :] = glong[:64]
         gls[:, 1, :] = glong[64:]
 
-        @pl.when(jnp.logical_not(hub))
+        slot = z * 4 + l % 4
+
+        def out_long():
+            @pl.when(jnp.logical_not(hub))
+            def _():
+                pl.semaphore_wait(ready, 1)
+
+            for dx, dy in OFFSETS:
+                d = 2 * chip_at(dx, dy)
+                out(gls.at[d], glr.at[slot], s3, r3, d, zo)
+                if (dx, dy) != (0, 0):
+                    out(gls.at[d + 1], glr.at[slot], s3, r3, d + 1, zo)
+
+            @pl.when(jnp.logical_not(hub))
+            def _():
+                out(gls.at[me], glr.at[slot], s3, r3, me, zo)
+
+            @pl.when(hub)
+            def _():
+                pltpu.make_async_copy(gls.at[me], glr.at[slot], r3).start()
+
+        @pl.when(z >= zo)
         def _():
-            pl.semaphore_wait(ready, 1)
-
-        slot = z * 4 + l % 4
-
-        def out3(d):
-            pltpu.make_async_remote_copy(
-                src_ref=gls.at[d],
-                dst_ref=glr.at[slot],
-                send_sem=s3,
-                recv_sem=r3,
-                device_id=(d, zo),
-                device_id_type=MESH,
-            ).start()
-
-        for dx, dy in OFFSETS:
-            chip = chip_at(dx, dy)
-            out3(2 * chip)
-            if (dx, dy) != (0, 0):
-                out3(2 * chip + 1)
-
-        @pl.when(jnp.logical_not(hub))
-        def _():
-            out3(me)
-
-        @pl.when(hub)
-        def _():
-            pltpu.make_async_copy(gls.at[me], glr.at[slot], r3).start()
-
-        h = forward(both(4))
+            out_long()
+
+        pltpu.make_async_copy(recv_f, recv_f, r4).wait()
+        h = forward(jnp.concatenate([recv_f[:, 0, :], recv_f[:, 1, :]], 0))
         hr, hi = h[:, :W], h[:, W:]
-        out = inverse(
+        both = inverse(
             jnp.concatenate(
                 [
                     jnp.concatenate([mr * hr - mi * hi, mr * hi + mi * hr], 1),
@@ -268,7 +271,7 @@
                 0,
             )
         )
-        recon, gmix = out[:, :W], out[:, W:]
+        recon, gmix = both[:, :W], both[:, W:]
         ge, gd = gmix[:64], gmix[64:]
         ge_next = jnp.where(half_row == 63, 0.0, pltpu.roll(ge, 63, 0))
         gms = split(gmix)
@@ -286,32 +289,28 @@
         for r in range(4, 8):
             ret[pl.ds(r, 64, stride=8), :] = jnp.broadcast_to(gmid, (64, W))
 
-        def out2(d):
-            pltpu.make_async_remote_copy(
-                src_ref=tile(ret, d),
-                dst_ref=tile(back, l),
-                send_sem=s2,
-                recv_sem=r2,
-                device_id=(d, z),
-                device_id_type=MESH,
-            ).start()
-
         for dx, dy in OFFSETS:
-            chip = chip_at(dx, dy)
-            out2(2 * chip)
+            d = 2 * chip_at(dx, dy)
+            out(tile(ret, d), tile(back, l), s2, r2, d, z)
             if (dx, dy) != (0, 0):
-                out2(2 * chip + 1)
+                out(tile(ret, d + 1), tile(back, l), s2, r2, d + 1, z)
         pltpu.make_async_copy(tile(ret, me), tile(back, l), r2).start()
+
+        @pl.when(z < zo)
+        def _():
+            out_long()
 
     def left(ref, count, sem):
         part = ref.at[pl.ds(0, count)]
         pltpu.make_async_copy(part, part, sem).wait()
 
-    left(send, 31 * 8, s1)
+    left(send, 31, s1)
+    left(send_f, 31, s4)
 
     @pl.when(jnp.logical_not(works))
     def _():
-        left(send, 8, s1)
+        left(send, 1, s1)
+        left(send_f, 1, s4)
 
     @pl.when(works)
     def _():
@@ -373,15 +372,17 @@
             vm((32, W), f32),
             *[vm(t.shape, t.dtype) for t in tabs],
             *[vm(*o) for o in outs],
-            vm((32 * 8, W), f32),
-            vm((64 * 8, W), f32),
+            vm((32, 4, W), f32),
+            vm((64, 4, W), f32),
+            vm((32, 2, W), f32),
+            vm((64, 2, W), f32),
             vm((64 * 8, W), f32),
             vm((32 * 8, W), f32),
             vm((64, 2, W), f32),
             dma((6,)),
             dma((10,)),
             dma((4,)),
-            *[dma] * 6,
+            *[dma] * 8,
             pltpu.SemaphoreType.REGULAR,
         ],
         compiler_params=pltpu.CompilerParams(collective_id=0, has_side_effects=True),

time: 36.1 us -> 30.1 us (0.83)
  Pallas kernels: 35.1 us -> 29.1 us
    pallas_call x1, Pallas kernels: 33.7 us -> 27.6 us  [local(): pl.pallas_call(kernel, out_shape=[*shapes, jax.ShapeDtypeStruct((32, 2, W...]
where the time goes in v3:
time: 30.1 us; the launch traced here: 29.7 us
  Pallas kernels  29.1 us (97%)
  between operations  0.64 us (2%)
    pallas_call x1, Pallas kernels, local(): pl.pallas_call(kernel, out_shape=[*shapes, jax.ShapeDtypeStruct((32, 2, W...  27.6 us
    pallas_call x1, Pallas kernels, local(): pl.pallas_call(deliver, out_shape=[*shapes[:3], jax.ShapeDtypeStruct((4,...  1.46 us

profile of v3, /device:TPU:1, one launch (start us, length us, event | category | flops | bytes accessed | tf_op | source)
XLA Modules:
  0.0 29.7 jit_solution(16088288138565907885)
XLA Ops:
  0.6 27.6 %shard_map.191 = (bf16[32,256]{1,0:T(8,128)(2,1)}, bf16[32,256]{1,0:T(8,128)(2,1)}, bf16[32,256]{1,0:T(8,128)(2,1)}, f32[32,128]{1,0:T(8,128)}, f32[32,2,128]{2,1,0:T(2,128)}) custom-call(bf16[32,256]{1,0:T(8,128)(2,1)} %og_h.1, bf16[32,256]{1,0:T(8,128)(2,1)} %ig_h.1, bf16[32,256]{1,0:T(8,128)(2,1)} %va_h.1, bf16[32,256]{1,0:T(8,128)(2,1)} %go_h.1, ...), custom_call_target="tpu_custom_call" | custom-call | tf_op jit(solution)/shard_map/pallas_call | solution.py:364
  28.3 1.5 %shard_map.192 = (bf16[32,256]{1,0:T(8,128)(2,1)}, bf16[32,256]{1,0:T(8,128)(2,1)}, bf16[32,256]{1,0:T(8,128)(2,1)}, f32[4,256]{1,0:T(4,128)}, f32[32,128]{1,0:T(8,128)}) custom-call(bf16[32,256]{1,0:T(8,128)(2,1)} %get-tuple-element.10.a, bf16[32,256]{1,0:T(8,128)(2,1)} %get-tuple-element.11.b, bf16[32,256]{1,0:T(8,128)(2,1)} %get-tuple-element.12.c, ...), custom_call_target="tpu_custom_call" | custom-call | tf_op jit(solution)/shard_map/pallas_call | solution.py:390

commit v4 on v3

--- a/solution.py
+++ b/solution.py
@@ -13,6 +13,7 @@
 f32 = jnp.float32
 bf16 = jnp.bfloat16
 N = 16384
+VMEM_BYTES = 16 * 1024 * 1024
 W = 128
 
 
@@ -75,14 +76,11 @@
 
 def kernel(og_h, ig_h, va_h, go_h, lf_h, mf_h, *refs):
     tab_h = refs[:10]
-    outs_h = refs[10:14]
-    glr = refs[14]
+    (go_o, gi_o, gv_o, gm_o, glr) = refs[10:15]
     (og, ig, va, go, lf, mf) = refs[15:21]
     tab = refs[21:31]
-    outs = refs[31:35]
-    go_o, gi_o, gv_o, gm_o = outs
-    (send, recv, send_f, recv_f, ret, back, gls) = refs[35:42]
-    (in_sem, tab_sem, out_sem, s1, r1, s2, r2, s3, r3, s4, r4, ready) = refs[42:]
+    (send, recv, send_f, recv_f, ret, back, gls) = refs[31:38]
+    (in_sem, tab_sem, s1, r1, s2, r2, s3, r3, s4, r4, ready) = refs[38:]
 
     me = lax.axis_index("ctx")
     z = lax.axis_index("ch")
@@ -332,24 +330,24 @@
     gi_o[...] = (gprod * va[...].astype(f32)).astype(bf16)
     gv_o[...] = (gprod * ig[...].astype(f32)).astype(bf16)
     gm_o[...] = rows(4)
-    leave = [pltpu.make_async_copy(a, b, out_sem.at[i]) for i, (a, b) in enumerate(zip(outs, outs_h))]
-    for c in leave:
-        c.start()
-    for c in leave:
-        c.wait()
     pltpu.make_async_copy(glr, glr, r3).wait()
 
 
-def deliver(a, b, c, m, parts, a_o, b_o, c_o, gl_o, m_o):
-    a_o[...] = a[...]
-    b_o[...] = b[...]
-    c_o[...] = c[...]
-    m_o[...] = m[...]
+def deliver(a, b, c, m, parts, a_o, b_o, c_o, gl_o, m_o, gl, sem):
+    copies = [
+        pltpu.make_async_copy(x, y, sem.at[i])
+        for i, (x, y) in enumerate([(a, a_o), (b, b_o), (c, c_o), (m, m_o), (gl, gl_o)])
+    ]
+    for copy in copies[:4]:
+        copy.start()
     total = parts[0:4]
     for i in range(1, 8):
         total = total + parts[4 * i : 4 * i + 4]
-    gl_o[:, :W] = total[:, 0, :]
-    gl_o[:, W:] = total[:, 1, :]
+    gl[:, :W] = total[:, 0, :]
+    gl[:, W:] = total[:, 1, :]
+    copies[4].start()
+    for copy in copies:
+        copy.wait()
 
 
 def local(outer_gate, inner_gate, values, grad_out, long_filter, mid_filter):
@@ -361,17 +359,17 @@
     ins = (outer_gate, inner_gate, values, grad_out, long_filter, mid_filter)
     outs = [((32, 256), bf16)] * 3 + [((32, W), f32)]
     shapes = [jax.ShapeDtypeStruct(*o) for o in outs]
+    ins = [pltpu.with_memory_space_constraint(a, pltpu.HBM) for a in (*ins, *map(jnp.asarray, tabs))]
     results = pl.pallas_call(
         kernel,
-        out_shape=[*shapes, jax.ShapeDtypeStruct((32, 2, W), f32)],
+        out_shape=[*[vm(*o) for o in outs], vm((32, 2, W), f32)],
         in_specs=[hbm] * 16,
-        out_specs=[hbm] * 5,
+        out_specs=[vmem] * 5,
         scratch_shapes=[
             *[vm((32, 256), bf16)] * 4,
             vm((32, 256), f32),
             vm((32, W), f32),
             *[vm(t.shape, t.dtype) for t in tabs],
-            *[vm(*o) for o in outs],
             vm((32, 4, W), f32),
             vm((64, 4, W), f32),
             vm((32, 2, W), f32),
@@ -381,17 +379,20 @@
             vm((64, 2, W), f32),
             dma((6,)),
             dma((10,)),
-            dma((4,)),
             *[dma] * 8,
             pltpu.SemaphoreType.REGULAR,
         ],
-        compiler_params=pltpu.CompilerParams(collective_id=0, has_side_effects=True),
-    )(*ins, *[jnp.asarray(t) for t in tabs])
+        compiler_params=pltpu.CompilerParams(
+            collective_id=0, has_side_effects=True, vmem_limit_bytes=VMEM_BYTES
+        ),
+    )(*ins)
     return pl.pallas_call(
         deliver,
         out_shape=[*shapes[:3], jax.ShapeDtypeStruct((4, 256), f32), shapes[3]],
         in_specs=[vmem] * 5,
-        out_specs=[vmem] * 5,
+        out_specs=[hbm] * 5,
+        scratch_shapes=[vm((4, 256), f32), dma((5,))],
+        compiler_params=pltpu.CompilerParams(vmem_limit_bytes=VMEM_BYTES),
     )(*results)
 
 

time: 30.1 us -> 28.4 us (0.944)
  Pallas kernels: 29.1 us -> 27.5 us
    pallas_call x1, Pallas kernels: 1.46 us -> 0.67 us  [local(): pl.pallas_call(deliver, out_shape=[*shapes[:3], jax.ShapeDtypeStruct((4,...]
    pallas_call x1, Pallas kernels: 27.6 us -> 26.9 us  [local(): pl.pallas_call(kernel, out_shape=[*[vm(*o) for o in outs], vm((32, 2, W),...]
where the time goes in v4:
time: 28.4 us; the launch traced here: 28.2 us
  Pallas kernels  27.5 us (97%)
  between operations  0.64 us (2%)
    pallas_call x1, Pallas kernels, local(): pl.pallas_call(kernel, out_shape=[*[vm(*o) for o in outs], vm((32, 2, W),...  26.9 us
    pallas_call x1, Pallas kernels, local(): pl.pallas_call(deliver, out_shape=[*shapes[:3], jax.ShapeDtypeStruct((4,...  0.67 us

profile of v4, /device:TPU:1, one launch (start us, length us, event | category | flops | bytes accessed | tf_op | source)
XLA Modules:
  0.0 28.2 jit_solution(7420162718713196530)
XLA Ops:
  0.6 26.9 %shard_map.191 = (bf16[32,256]{1,0:T(8,128)(2,1)S(1)}, bf16[32,256]{1,0:T(8,128)(2,1)S(1)}, bf16[32,256]{1,0:T(8,128)(2,1)S(1)}, f32[32,128]{1,0:T(8,128)S(1)}, f32[32,2,128]{2,1,0:T(2,128)S(1)}) custom-call(bf16[32,256]{1,0:T(8,128)(2,1)} %og_h.1, bf16[32,256]{1,0:T(8,128)(2,1)} %ig_h.1, bf16[32,256]{1,0:T(8,128)(2,1)} %va_h.1, bf16[32,256]{1,0:T(8,128)(2,1)} %go_h.1, ...), custom_call_target="tpu_custom_call" | custom-call | tf_op jit(solution)/shard_map/pallas_call | solution.py:363
  27.5 0.7 %shard_map.192 = (bf16[32,256]{1,0:T(8,128)(2,1)}, bf16[32,256]{1,0:T(8,128)(2,1)}, bf16[32,256]{1,0:T(8,128)(2,1)}, f32[4,256]{1,0:T(4,128)}, f32[32,128]{1,0:T(8,128)}) custom-call(bf16[32,256]{1,0:T(8,128)(2,1)S(1)} %get-tuple-element.10.a, bf16[32,256]{1,0:T(8,128)(2,1)S(1)} %get-tuple-element.11.b, bf16[32,256]{1,0:T(8,128)(2,1)S(1)} %get-tuple-element.12.c, ...), custom_call_target="tpu_custom_call" | custom-call | tf_op jit(solution)/shard_map/pallas_call | solution.py:389

commit v5 on v4

v5 whole, which is shorter than its diff:
```python
import functools
import math

import jax
import jax.numpy as jnp
import numpy as np
from jax import lax
from jax.experimental import pallas as pl
from jax.experimental.pallas import tpu as pltpu
from jax.sharding import PartitionSpec as P

MESH = pl.DeviceIdType.MESH
f32 = jnp.float32
bf16 = jnp.bfloat16
N = 16384
LEAD = 3
VMEM_BYTES = 16 * 1024 * 1024
W = 128


def split_np(a):
    a = np.asarray(a, np.float32)
    hi = a.astype(jnp.bfloat16)
    lo = (a - hi.astype(np.float32)).astype(jnp.bfloat16)
    return hi, lo


def tables():
    order = np.concatenate([np.arange(0, W, 2), np.arange(1, W, 2)]).astype(np.float64)
    k = np.arange(W, dtype=np.float64)
    ang = 2.0 * math.pi * (k + 0.5)[:, None] * order[None, :] / (2 * W)
    w1 = np.concatenate([np.cos(ang), -np.sin(ang)], 0)
    w1i = w1.T / N
    tw = 2.0 * math.pi * (k + 0.5)[:, None] * k[None, :] / (2 * N)
    tc, ts = np.cos(tw), np.sin(tw)
    a2 = 2.0 * math.pi * ((k[:, None] * k[None, :]) % W) / W
    c, s = np.cos(a2), np.sin(a2)
    w2 = np.block([[c, -s], [s, c]])
    (w1h, w1l), (w2h, w2l), (w3h, w3l), (w4h, w4l) = map(split_np, (w1, w2, w2.T, w1i))
    return (
        np.concatenate([w1h, w1h, w1l], 1),
        np.concatenate([w2h, w2h, w2l], 0),
        np.concatenate([w3h, w3h, w3l], 0),
        np.concatenate([w4h, w4h, w4l], 1),
        tc.astype(np.float32),
        ts.astype(np.float32),
    )


def split(a):
    hi = a.astype(bf16)
    lo = (a - hi.astype(f32)).astype(bf16)
    return hi, lo


def dot(a, b, dims=(((1,), (0,)), ((), ()))):
    return lax.dot_general(a, b, dims, preferred_element_type=f32)


def data(parts, axis):
    hi, lo = zip(*parts)
    return jnp.concatenate([*hi, *lo, *hi], axis)


def taps(parts, axis):
    hi, lo = zip(*parts)
    return jnp.concatenate([*hi, *hi, *lo], axis)


NT = (((1,), (1,)), ((), ()))
TN = (((0,), (0,)), ((), ()))


def ring(d, n):
    return min(d, n - d)


OFFSETS = sorted(
    [(dx, dy) for dx in range(4) for dy in range(8)], key=lambda o: -(ring(o[0], 4) + ring(o[1], 8))
)


def kernel(og_h, ig_h, va_h, go_h, lf_h, mf_h, *refs):
    tab_h = refs[:6]
    (go_o, gi_o, gv_o, gm_o, glr) = refs[6:11]
    (og, ig, va, go, lf, mf) = refs[11:17]
    tab = refs[17:23]
    (send, recv, send_f, recv_f, ret, back, gls) = refs[23:30]
    (in_sem, tab_sem, s1, r1, s2, r2, s3, r3, s4, r4, ready, here, near, far) = refs[30:]

    me = lax.axis_index("ctx")
    z = lax.axis_index("ch")
    chip = me // 2
    core = me % 2
    px, py = chip // 8, chip % 8

    def channel(c):
        x, y = c // 8, c % 8
        return jnp.where(y < LEAD, LEAD * x + y, (8 - LEAD) * x + y + 3 * LEAD)

    works = core == 1
    leads = py < LEAD
    l = channel(chip)
    zo = l // 4
    hub = z == zo
    told = jnp.logical_and(zo < LEAD, z >= 4)
    bar = pltpu.get_barrier_semaphore()

    def signal(sem, ctx, ch):
        pl.semaphore_signal(sem, inc=1, device_id=(ctx, ch), device_id_type=MESH)

    def chip_at(dx, dy):
        return lax.rem(px + dx, 4) * 8 + lax.rem(py + dy, 8)

    ins = [
        pltpu.make_async_copy(a, b, in_sem.at[i])
        for i, (a, b) in enumerate(
            [(ig_h, ig), (va_h, va), (go_h, go), (og_h, og), (lf_h, lf), (mf_h, mf)]
        )
    ]
    for c in ins:
        c.start()
    tabs = [pltpu.make_async_copy(a, b, tab_sem.at[i]) for i, (a, b) in enumerate(zip(tab_h, tab))]

    @pl.when(core == 0)
    def _():
        signal(bar, me + 1, z)

    @pl.when(z < LEAD)
    def _():
        for p in (4, 5, 6, 7):
            for i in range(4):
                g = 4 * z + i
                signal(bar, 2 * ((g // LEAD) * 8 + g % LEAD) + 1, p)

    @pl.when(works)
    def _():
        for dx, dy in OFFSETS[:-1]:
            signal(bar, 2 * chip_at(dx, dy) + jnp.where(leads, 1, 0), z)

        @pl.when(jnp.logical_not(leads))
        def _():
            signal(bar, me - 1, z)

        @pl.when(z < zo)
        def _():
            signal(bar, me, zo)

        @pl.when(hub)
        def _():
            for p in range(1, 8):
                above = z < p if p < 4 else jnp.logical_and(z < p, z >= LEAD)

                @pl.when(above)
                def _():
                    signal(bar, me, p)

        for c in tabs:
            c.start()

    for c in ins:
        c.wait()

    product = ig[...].astype(f32) * va[...].astype(f32)
    conv = go[...].astype(f32) * og[...].astype(f32)
    filt = lf[...]
    send[:, 0, :] = product[:, :W]
    send[:, 1, :] = product[:, W:]
    send[:, 2, :] = conv[:, :W]
    send[:, 3, :] = conv[:, W:]
    send_f[:, 0, :] = filt[:, :W]
    send_f[:, 1, :] = filt[:, W:]

    def out(src, dst, ssem, rsem, d, p):
        pltpu.make_async_remote_copy(
            src_ref=src,
            dst_ref=dst,
            send_sem=ssem,
            recv_sem=rsem,
            device_id=(d, p),
            device_id_type=MESH,
        ).start()

    def put_all(src, dst, ssem, rsem, lead):
        def put(c):
            out(src.at[channel(c)], dst.at[me], ssem, rsem, 2 * c + 1, z)

        for off in OFFSETS:
            c = chip_at(*off)
            mine = (c % 8 < LEAD) == lead
            if off == (0, 0):
                mine = jnp.logical_and(mine, core == 0)
            pl.when(mine)(functools.partial(put, c))

    @pl.when(works)
    def _():
        from_below = jnp.where(hub, zo, jnp.where(z > zo, jnp.where(told, 64, 1), 0))
        pl.semaphore_wait(bar, 4 * LEAD + 1 - jnp.where(leads, 1, 0) + from_below)
        signal(near, me - 1, z)

        @pl.when(jnp.logical_and(z > zo, jnp.logical_not(told)))
        def _():
            signal(here, me, zo)

    @pl.when(core == 0)
    def _():
        pl.semaphore_wait(near, 1)

    put_all(send, recv, s1, r1, True)

    @pl.when(core == 0)
    def _():
        pl.semaphore_wait(bar, 32 - 4 * LEAD)
        signal(far, me + 1, z)

    @pl.when(works)
    def _():
        pl.semaphore_wait(far, 1)

    put_all(send, recv, s1, r1, False)
    put_all(send_f, recv_f, s4, r4, True)
    put_all(send_f, recv_f, s4, r4, False)

    @pl.when(works)
    def _():
        pltpu.make_async_copy(send.at[l], recv.at[me], r1).start()
        pltpu.make_async_copy(send_f.at[l], recv_f.at[me], r4).start()

        for c in tabs:
            c.wait()
        (w1, w2, w3, w4, tcr, tsr) = tab
        tc, ts = tcr[...], tsr[...]
        row = lax.broadcasted_iota(jnp.int32, (W, W), 0)
        col = lax.broadcasted_iota(jnp.int32, (W, W), 1)
        upper = col >= row
        half_row = lax.broadcasted_iota(jnp.int32, (64, W), 0)
        k = jnp.broadcast_to(mf[pl.ds(l, 1), :], (W, W))
        rolled = pltpu.roll(k, 0, 1, stride=1, stride_axis=0)
        k0 = split(jnp.where(upper, rolled, 0.0))
        k1 = split(jnp.where(upper, 0.0, rolled))

        pltpu.make_async_copy(recv, recv, r1).wait()

        @pl.when(hub)
        def _():
            for p in range(7):
                @pl.when(p < z)
                def _():
                    signal(ready, me, p)

        def ready_above():
            top = jnp.where(zo < LEAD, 3, 7)

            @pl.when(z < top)
            def _():
                pl.semaphore_wait(here, top - z)

            for p in range(7, 0, -1):
                @pl.when(jnp.logical_and(z < p, p <= top))
                def _():
                    signal(ready, me, p)

        def forward(x):
            s = dot(w1[...], data([split(x)], 0))
            re, im = s[:W], s[W:]
            t = jnp.concatenate([re * tc + im * ts, im * tc - re * ts], 1)
            t = dot(data([split(t)], 1), w2[...])
            return t[:, :W], t[:, W:]

        def inverse(y):
            t = dot(data([split(y)], 1), w3[...])
            parts = []
            for i in range(y.shape[0] // W):
                re, im = t[i * W : (i + 1) * W, :W], t[i * W : (i + 1) * W, W:]
                parts.append(jnp.concatenate([re * tc - im * ts, im * tc + re * ts], 0))
            return dot(w4[...], data([split(jnp.concatenate(parts, 1))], 0))

        def times(a, b):
            return jnp.concatenate([a[0] * b[0] - a[1] * b[1], a[0] * b[1] + a[1] * b[0]], 1)

        def times_conj(a, b):
            return jnp.concatenate([a[0] * b[0] + a[1] * b[1], a[1] * b[0] - a[0] * b[1]], 1)

        c = forward(jnp.concatenate([recv[:, 2, :], recv[:, 3, :]], 0))
        pe, po = recv[:, 0, :], recv[:, 1, :]
        po_prev = jnp.where(half_row == 0, 0.0, pltpu.roll(po, 1, 0))
        p0 = split(jnp.concatenate([pe, po], 0))
        p1 = split(jnp.concatenate([po_prev, pe], 0))
        m = forward(dot(data([p0, p1], 1), taps([k0, k1], 0)))
        glong = inverse(times_conj(c, m)) * (N**-0.5)
        gls[:, 0, :] = glong[:64]
        gls[:, 1, :] = glong[64:]

        slot = z * 4 + l % 4

        def out_long():
            @pl.when(jnp.logical_not(jnp.logical_or(hub, told)))
            def _():
                pl.semaphore_wait(ready, 1)

            for dx, dy in OFFSETS:
                d = 2 * chip_at(dx, dy)
                out(gls.at[d + 1 - core], glr.at[slot], s3, r3, d + 1 - core, zo)
                if (dx, dy) != (0, 0):
                    out(gls.at[d + core], glr.at[slot], s3, r3, d + core, zo)

            @pl.when(jnp.logical_not(hub))
            def _():
                out(gls.at[me], glr.at[slot], s3, r3, me, zo)

            @pl.when(hub)
            def _():
                pltpu.make_async_copy(gls.at[me], glr.at[slot], r3).start()

        @pl.when(z >= zo)
        def _():
            @pl.when(jnp.logical_and(hub, zo >= LEAD))
            def _():
                ready_above()

            out_long()

            @pl.when(jnp.logical_and(hub, zo < LEAD))
            def _():
                ready_above()

        pltpu.make_async_copy(recv_f, recv_f, r4).wait()
        h = forward(jnp.concatenate([recv_f[:, 0, :], recv_f[:, 1, :]], 0))
        both = inverse(jnp.concatenate([times(m, h), times_conj(c, h)], 0))
        recon, gmix = both[:, :W], both[:, W:]
        ge, gd = gmix[:64], gmix[64:]
        ge_next = jnp.where(half_row == 63, 0.0, pltpu.roll(ge, 63, 0))
        g0 = split(gmix)
        g1 = split(jnp.concatenate([gd, ge_next], 0))
        gprod = dot(data([g0, g1], 1), taps([k0, k1], 1), NT)
        g3 = taps([g0], 0)
        d = jnp.where(upper, dot(data([p0], 0), g3, TN), dot(data([p1], 0), g3, TN))
        for bit in range(7):
            moved = pltpu.roll(d, W - (1 << bit), 1)
            d = jnp.where((row >> bit) & 1 == 1, moved, d)
        gmid = jnp.sum(d, 0, keepdims=True) * (N**-0.5)

        ret[:, 0, :] = recon[:64]
        ret[:, 1, :] = recon[64:]
        ret[:, 2, :] = gprod[:64]
        ret[:, 3, :] = gprod[64:]
        ret[:, 4, :] = jnp.broadcast_to(gmid, (64, W))

        for dx, dy in OFFSETS:
            d = 2 * chip_at(dx, dy)
            out(ret.at[d + 1 - core], back.at[l], s2, r2, d + 1 - core, z)
            if (dx, dy) != (0, 0):
                out(ret.at[d + core], back.at[l], s2, r2, d + core, z)
        pltpu.make_async_copy(ret.at[me], back.at[l], r2).start()

        @pl.when(z < zo)
        def _():
            out_long()

    def left(ref, count, sem):
        part = ref.at[pl.ds(0, count)]
        pltpu.make_async_copy(part, part, sem).wait()

    left(send, 31, s1)
    left(send_f, 31, s4)

    @pl.when(jnp.logical_not(works))
    def _():
        left(send, 1, s1)
        left(send_f, 1, s4)

    @pl.when(works)
    def _():
        left(gls, 63, s3)
        left(ret, 63, s2)

        @pl.when(jnp.logical_not(hub))
        def _():
            left(gls, 1, s3)

    pltpu.make_async_copy(back, back, r2).wait()
    recon = jnp.concatenate([back[:, 0, :], back[:, 1, :]], 1)
    gprod = jnp.concatenate([back[:, 2, :], back[:, 3, :]], 1)
    go_o[...] = (go[...].astype(f32) * recon).astype(bf16)
    gi_o[...] = (gprod * va[...].astype(f32)).astype(bf16)
    gv_o[...] = (gprod * ig[...].astype(f32)).astype(bf16)
    gm_o[...] = back[:, 4, :]
    pltpu.make_async_copy(glr, glr, r3).wait()


def deliver(a, b, c, m, parts, a_o, b_o, c_o, gl_o, m_o, gl, sem):
    copies = [
        pltpu.make_async_copy(x, y, sem.at[i])
        for i, (x, y) in enumerate([(a, a_o), (b, b_o), (c, c_o), (m, m_o), (gl, gl_o)])
    ]
    for copy in copies[:4]:
        copy.start()
    total = parts[0:4]
    for i in range(1, 8):
        total = total + parts[4 * i : 4 * i + 4]
    gl[:, :W] = total[:, 0, :]
    gl[:, W:] = total[:, 1, :]
    copies[4].start()
    for copy in copies:
        copy.wait()


def local(outer_gate, inner_gate, values, grad_out, long_filter, mid_filter):
    tabs = tables()
    vm = pltpu.VMEM
    dma = pltpu.SemaphoreType.DMA
    hbm = pl.BlockSpec(memory_space=pl.ANY)
    vmem = pl.BlockSpec(memory_space=vm)
    ins = (outer_gate, inner_gate, values, grad_out, long_filter, mid_filter)
    outs = [((32, 256), bf16)] * 3 + [((32, W), f32)]
    shapes = [jax.ShapeDtypeStruct(*o) for o in outs]
    ins = [pltpu.with_memory_space_constraint(a, pltpu.HBM) for a in (*ins, *map(jnp.asarray, tabs))]
    results = pl.pallas_call(
        kernel,
        out_shape=[*[vm(*o) for o in outs], vm((32, 2, W), f32)],
        in_specs=[hbm] * 12,
        out_specs=[vmem] * 5,
        scratch_shapes=[
            *[vm((32, 256), bf16)] * 4,
            vm((32, 256), f32),
            vm((32, W), f32),
            *[vm(t.shape, t.dtype) for t in tabs],
            vm((32, 4, W), f32),
            vm((64, 4, W), f32),
            vm((32, 2, W), f32),
            vm((64, 2, W), f32),
            vm((64, 5, W), f32),
            vm((32, 5, W), f32),
            vm((64, 2, W), f32),
            dma((6,)),
            dma((6,)),
            *[dma] * 8,
            *[pltpu.SemaphoreType.REGULAR] * 4,
        ],
        compiler_params=pltpu.CompilerParams(
            collective_id=0, has_side_effects=True, vmem_limit_bytes=VMEM_BYTES
        ),
    )(*ins)
    return pl.pallas_call(
        deliver,
        out_shape=[*shapes[:3], jax.ShapeDtypeStruct((4, 256), f32), shapes[3]],
        in_specs=[vmem] * 5,
        out_specs=[hbm] * 5,
        scratch_shapes=[vm((4, 256), f32), dma((5,))],
        compiler_params=pltpu.CompilerParams(vmem_limit_bytes=VMEM_BYTES),
    )(*results)


def solution(mesh):
    in_specs = (
        P("ch", "ctx"),
        P("ch", "ctx"),
        P("ch", "ctx"),
        P("ch", "ctx"),
        P(None, "ctx"),
        P("ch", None),
    )
    out_specs = (P("ch", "ctx"), P("ch", "ctx"), P("ch", "ctx"), P("ch", "ctx"), P("ch", None))
    return jax.shard_map(local, mesh=mesh, in_specs=in_specs, out_specs=out_specs, check_vma=False)
```

time: 28.4 us -> 27.2 us (0.958)
  Pallas kernels: 27.5 us -> 26.3 us
    pallas_call x1, Pallas kernels: 26.9 us -> 25.7 us  [local(): pl.pallas_call(kernel, out_shape=[*[vm(*o) for o in outs], vm((32, 2, W),...]
where the time goes in v5:
time: 27.2 us; the launch traced here: 27 us
  Pallas kernels  26.3 us (97%)
  between operations  0.64 us (2%)
    pallas_call x1, Pallas kernels, local(): pl.pallas_call(kernel, out_shape=[*[vm(*o) for o in outs], vm((32, 2, W),...  25.7 us
    pallas_call x1, Pallas kernels, local(): pl.pallas_call(deliver, out_shape=[*shapes[:3], jax.ShapeDtypeStruct((4,...  0.67 us

profile of v5, /device:TPU:1, one launch (start us, length us, event | category | flops | bytes accessed | tf_op | source)
XLA Modules:
  0.0 27.0 jit_solution(4343122902627817006)
XLA Ops:
  0.6 25.7 %shard_map.155 = (bf16[32,256]{1,0:T(8,128)(2,1)S(1)}, bf16[32,256]{1,0:T(8,128)(2,1)S(1)}, bf16[32,256]{1,0:T(8,128)(2,1)S(1)}, f32[32,128]{1,0:T(8,128)S(1)}, f32[32,2,128]{2,1,0:T(2,128)S(1)}) custom-call(bf16[32,256]{1,0:T(8,128)(2,1)} %og_h.1, bf16[32,256]{1,0:T(8,128)(2,1)} %ig_h.1, bf16[32,256]{1,0:T(8,128)(2,1)} %va_h.1, bf16[32,256]{1,0:T(8,128)(2,1)} %go_h.1, ...), custom_call_target="tpu_custom_call" | custom-call | tf_op jit(solution)/shard_map/pallas_call | solution.py:418
  26.3 0.7 %shard_map.156 = (bf16[32,256]{1,0:T(8,128)(2,1)}, bf16[32,256]{1,0:T(8,128)(2,1)}, bf16[32,256]{1,0:T(8,128)(2,1)}, f32[4,256]{1,0:T(4,128)}, f32[32,128]{1,0:T(8,128)}) custom-call(bf16[32,256]{1,0:T(8,128)(2,1)S(1)} %get-tuple-element.10.a, bf16[32,256]{1,0:T(8,128)(2,1)S(1)} %get-tuple-element.11.b, bf16[32,256]{1,0:T(8,128)(2,1)S(1)} %get-tuple-element.12.c, ...), custom_call_target="tpu_custom_call" | custom-call | tf_op jit(solution)/shard_map/pallas_call | solution.py:444

commit v6 on v5

--- a/solution.py
+++ b/solution.py
@@ -13,7 +13,9 @@
 f32 = jnp.float32
 bf16 = jnp.bfloat16
 N = 16384
-LEAD = 3
+LEAD = 12
+DIRECT = 2
+TOLD = 4
 VMEM_BYTES = 16 * 1024 * 1024
 W = 128
 
@@ -80,6 +82,28 @@
 )
 
 
+CHIPS = [x * 8 + y for x, y in reversed(OFFSETS)]
+
+
+PLACES = [
+    *[(0, 0), (0, 1), (1, 0), (3, 0)],
+    *[(1, 1), (3, 1), (2, 0), (2, 1)],
+    *[(0, 7), (0, 2), (1, 2), (0, 3)],
+    *[(1, 7), (3, 7), (0, 6), (3, 2)],
+    *[(0, 5), (0, 4), (2, 5), (2, 4)],
+    *[(3, 6), (3, 3), (2, 6), (3, 4)],
+    *[(1, 6), (1, 3), (3, 5), (1, 4)],
+    *[(2, 7), (2, 2), (1, 5), (2, 3)],
+]
+
+
+def pick(i, values):
+    if len(values) == 1:
+        return values[0]
+    half = len(values) // 2
+    return jnp.where(i < half, pick(i, values[:half]), pick(i - half, values[half:]))
+
+
 def kernel(og_h, ig_h, va_h, go_h, lf_h, mf_h, *refs):
     tab_h = refs[:6]
     (go_o, gi_o, gv_o, gm_o, glr) = refs[6:11]
@@ -94,16 +118,15 @@
     core = me % 2
     px, py = chip // 8, chip % 8
 
-    def channel(c):
-        x, y = c // 8, c % 8
-        return jnp.where(y < LEAD, LEAD * x + y, (8 - LEAD) * x + y + 3 * LEAD)
+    def channel(x, y):
+        return pick(x, [PLACES.index((i, y)) for i in range(4)])
 
     works = core == 1
-    leads = py < LEAD
-    l = channel(chip)
+    l = pick(py, [channel(px, y) for y in range(8)])
+    leads = l < LEAD
     zo = l // 4
     hub = z == zo
-    told = jnp.logical_and(zo < LEAD, z >= 4)
+    told = jnp.logical_and(zo < TOLD, z >= TOLD)
     bar = pltpu.get_barrier_semaphore()
 
     def signal(sem, ctx, ch):
@@ -111,6 +134,33 @@
 
     def chip_at(dx, dy):
         return lax.rem(px + dx, 4) * 8 + lax.rem(py + dy, 8)
+
+    @pl.when(core == 0)
+    def _():
+        signal(bar, me + 1, z)
+
+    @pl.when(works)
+    def _():
+        for dx, dy in OFFSETS[:-1]:
+            signal(bar, 2 * chip_at(dx, dy) + jnp.where(leads, 1, 0), z)
+
+        @pl.when(jnp.logical_not(leads))
+        def _():
+            signal(bar, me - 1, z)
+
+        @pl.when(z < zo)
+        def _():
+            signal(bar, me, zo)
+
+        @pl.when(hub)
+        def _():
+            for p in range(1, 8):
+                above = z < p if p < TOLD else jnp.logical_and(z < p, z >= TOLD)
+
+                @pl.when(above)
+                def _():
+                    signal(bar, me, p)
+
 
     ins = [
         pltpu.make_async_copy(a, b, in_sem.at[i])
@@ -122,54 +172,37 @@
         c.start()
     tabs = [pltpu.make_async_copy(a, b, tab_sem.at[i]) for i, (a, b) in enumerate(zip(tab_h, tab))]
 
-    @pl.when(core == 0)
-    def _():
-        signal(bar, me + 1, z)
-
-    @pl.when(z < LEAD)
-    def _():
-        for p in (4, 5, 6, 7):
+    @pl.when(z < TOLD)
+    def _():
+        for p in range(TOLD, 8):
             for i in range(4):
-                g = 4 * z + i
-                signal(bar, 2 * ((g // LEAD) * 8 + g % LEAD) + 1, p)
-
-    @pl.when(works)
-    def _():
-        for dx, dy in OFFSETS[:-1]:
-            signal(bar, 2 * chip_at(dx, dy) + jnp.where(leads, 1, 0), z)
-
-        @pl.when(jnp.logical_not(leads))
-        def _():
-            signal(bar, me - 1, z)
-
-        @pl.when(z < zo)
-        def _():
-            signal(bar, me, zo)
-
-        @pl.when(hub)
-        def _():
-            for p in range(1, 8):
-                above = z < p if p < 4 else jnp.logical_and(z < p, z >= LEAD)
-
-                @pl.when(above)
-                def _():
-                    signal(bar, me, p)
-
+                at = [PLACES[4 * q + i] for q in range(TOLD)]
+                signal(bar, pick(z, [2 * (8 * x + y) + (1 if q < DIRECT else 0) for q, (x, y) in enumerate(at)]), p)
+
+    @pl.when(works)
+    def _():
         for c in tabs:
             c.start()
 
-    for c in ins:
+    for c in ins[:4]:
         c.wait()
 
     product = ig[...].astype(f32) * va[...].astype(f32)
     conv = go[...].astype(f32) * og[...].astype(f32)
-    filt = lf[...]
     send[:, 0, :] = product[:, :W]
     send[:, 1, :] = product[:, W:]
     send[:, 2, :] = conv[:, :W]
     send[:, 3, :] = conv[:, W:]
-    send_f[:, 0, :] = filt[:, :W]
-    send_f[:, 1, :] = filt[:, W:]
+
+    @pl.when(works)
+    def _():
+        from_below = jnp.where(hub, zo, jnp.where(z > zo, jnp.where(told, jnp.where(zo < DIRECT, 64, 0), 1), 0))
+        pl.semaphore_wait(bar, LEAD + 1 - jnp.where(leads, 1, 0) + from_below)
+        signal(near, me - 1, z)
+
+        @pl.when(jnp.logical_and(z > zo, jnp.logical_not(told)))
+        def _():
+            signal(here, me, zo)
 
     def out(src, dst, ssem, rsem, d, p):
         pltpu.make_async_remote_copy(
@@ -181,45 +214,47 @@
             device_id_type=MESH,
         ).start()
 
-    def put_all(src, dst, ssem, rsem, lead):
-        def put(c):
-            out(src.at[channel(c)], dst.at[me], ssem, rsem, 2 * c + 1, z)
-
-        for off in OFFSETS:
-            c = chip_at(*off)
-            mine = (c % 8 < LEAD) == lead
-            if off == (0, 0):
-                mine = jnp.logical_and(mine, core == 0)
-            pl.when(mine)(functools.partial(put, c))
-
-    @pl.when(works)
-    def _():
-        from_below = jnp.where(hub, zo, jnp.where(z > zo, jnp.where(told, 64, 1), 0))
-        pl.semaphore_wait(bar, 4 * LEAD + 1 - jnp.where(leads, 1, 0) + from_below)
-        signal(near, me - 1, z)
-
-        @pl.when(jnp.logical_and(z > zo, jnp.logical_not(told)))
-        def _():
-            signal(here, me, zo)
+    def put_all(src, dst, ssem, rsem, channels):
+        def put(x, y):
+            out(src.at[channel(x, y)], dst.at[me], ssem, rsem, 2 * (8 * x + y) + 1, z)
+
+        def put_near(x, y):
+            mine = jnp.logical_and(works, jnp.logical_and(px == x, py == y))
+            pl.when(jnp.logical_not(mine))(functools.partial(put, x, y))
+
+        chips = [PLACES[i] for i in channels]
+        rows = [y for y in range(8) if all((x, y) in chips for x in range(4))]
+        for dx in (2, 1, 3):
+            for y in rows:
+                put(lax.rem(px + dx, 4), y)
+        for y in rows:
+            put_near(px, y)
+        for x, y in chips:
+            if y not in rows:
+                put_near(x, y)
 
     @pl.when(core == 0)
     def _():
         pl.semaphore_wait(near, 1)
 
-    put_all(send, recv, s1, r1, True)
+    put_all(send, recv, s1, r1, range(LEAD))
 
     @pl.when(core == 0)
     def _():
-        pl.semaphore_wait(bar, 32 - 4 * LEAD)
+        pl.semaphore_wait(bar, 32 - LEAD + jnp.where(jnp.logical_and(told, zo >= DIRECT), 64, 0))
         signal(far, me + 1, z)
 
     @pl.when(works)
     def _():
         pl.semaphore_wait(far, 1)
 
-    put_all(send, recv, s1, r1, False)
-    put_all(send_f, recv_f, s4, r4, True)
-    put_all(send_f, recv_f, s4, r4, False)
+    put_all(send, recv, s1, r1, range(LEAD, 32))
+    for c in ins[4:]:
+        c.wait()
+    filt = lf[...]
+    send_f[:, 0, :] = filt[:, :W]
+    send_f[:, 1, :] = filt[:, W:]
+    put_all(send_f, recv_f, s4, r4, range(32))
 
     @pl.when(works)
     def _():
@@ -249,7 +284,7 @@
                     signal(ready, me, p)
 
         def ready_above():
-            top = jnp.where(zo < LEAD, 3, 7)
+            top = jnp.where(zo < TOLD, TOLD - 1, 7)
 
             @pl.when(z < top)
             def _():
@@ -259,6 +294,8 @@
                 @pl.when(jnp.logical_and(z < p, p <= top))
                 def _():
                     signal(ready, me, p)
+
+        pl.when(jnp.logical_and(hub, zo >= TOLD))(ready_above)
 
         def forward(x):
             s = dot(w1[...], data([split(x)], 0))
@@ -287,42 +324,32 @@
         p0 = split(jnp.concatenate([pe, po], 0))
         p1 = split(jnp.concatenate([po_prev, pe], 0))
         m = forward(dot(data([p0, p1], 1), taps([k0, k1], 0)))
-        glong = inverse(times_conj(c, m)) * (N**-0.5)
-        gls[:, 0, :] = glong[:64]
-        gls[:, 1, :] = glong[64:]
-
         slot = z * 4 + l % 4
 
-        def out_long():
+        def long_gradient():
+            glong = inverse(times_conj(c, m)) * (N**-0.5)
+            gls[:, 0, :] = glong[:64]
+            gls[:, 1, :] = glong[64:]
+
             @pl.when(jnp.logical_not(jnp.logical_or(hub, told)))
             def _():
                 pl.semaphore_wait(ready, 1)
 
-            for dx, dy in OFFSETS:
-                d = 2 * chip_at(dx, dy)
-                out(gls.at[d + 1 - core], glr.at[slot], s3, r3, d + 1 - core, zo)
-                if (dx, dy) != (0, 0):
-                    out(gls.at[d + core], glr.at[slot], s3, r3, d + core, zo)
-
-            @pl.when(jnp.logical_not(hub))
-            def _():
-                out(gls.at[me], glr.at[slot], s3, r3, me, zo)
+            def put(d):
+                out(gls.at[d], glr.at[slot], s3, r3, d, zo)
+
+            for i in CHIPS:
+                put(2 * i + 1 - core)
+                pl.when(jnp.logical_not(jnp.logical_and(hub, chip == i)))(
+                    functools.partial(put, 2 * i + core)
+                )
 
             @pl.when(hub)
             def _():
                 pltpu.make_async_copy(gls.at[me], glr.at[slot], r3).start()
 
-        @pl.when(z >= zo)
-        def _():
-            @pl.when(jnp.logical_and(hub, zo >= LEAD))
-            def _():
-                ready_above()
-
-            out_long()
-
-            @pl.when(jnp.logical_and(hub, zo < LEAD))
-            def _():
-                ready_above()
+        soon = jnp.logical_and(z >= zo, z >= 3)
+        pl.when(soon)(long_gradient)
 
         pltpu.make_async_copy(recv_f, recv_f, r4).wait()
         h = forward(jnp.concatenate([recv_f[:, 0, :], recv_f[:, 1, :]], 0))
@@ -346,16 +373,16 @@
         ret[:, 3, :] = gprod[64:]
         ret[:, 4, :] = jnp.broadcast_to(gmid, (64, W))
 
-        for dx, dy in OFFSETS:
-            d = 2 * chip_at(dx, dy)
-            out(ret.at[d + 1 - core], back.at[l], s2, r2, d + 1 - core, z)
-            if (dx, dy) != (0, 0):
-                out(ret.at[d + core], back.at[l], s2, r2, d + core, z)
+        def put_back(d):
+            out(ret.at[d], back.at[l], s2, r2, d, z)
+
+        for i in CHIPS:
+            put_back(2 * i + 1 - core)
+            pl.when(chip != i)(functools.partial(put_back, 2 * i + core))
         pltpu.make_async_copy(ret.at[me], back.at[l], r2).start()
 
-        @pl.when(z < zo)
-        def _():
-            out_long()
+        pl.when(jnp.logical_and(hub, zo < TOLD))(ready_above)
+        pl.when(jnp.logical_not(soon))(long_gradient)
 
     def left(ref, count, sem):
         part = ref.at[pl.ds(0, count)]

time: 27.2 us -> 26.7 us (0.982)
  Pallas kernels: 26.3 us -> 25.7 us
    pallas_call x1, Pallas kernels: 25.7 us -> 25 us  [local(): pl.pallas_call(kernel, out_shape=[*[vm(*o) for o in outs], vm((32, 2, W),...]
where the time goes in v6:
time: 26.7 us; the launch traced here: 26.4 us
  Pallas kernels  25.7 us (96%)
  between operations  0.64 us (2%)
    pallas_call x1, Pallas kernels, local(): pl.pallas_call(kernel, out_shape=[*[vm(*o) for o in outs], vm((32, 2, W),...  25 us
    pallas_call x1, Pallas kernels, local(): pl.pallas_call(deliver, out_shape=[*shapes[:3], jax.ShapeDtypeStruct((4,...  0.67 us

profile of v6, /device:TPU:1, one launch (start us, length us, event | category | flops | bytes accessed | tf_op | source)
XLA Modules:
  0.0 26.4 jit_solution(5050850483174755116)
XLA Ops:
  0.6 25.0 %shard_map.155 = (bf16[32,256]{1,0:T(8,128)(2,1)S(1)}, bf16[32,256]{1,0:T(8,128)(2,1)S(1)}, bf16[32,256]{1,0:T(8,128)(2,1)S(1)}, f32[32,128]{1,0:T(8,128)S(1)}, f32[32,2,128]{2,1,0:T(2,128)S(1)}) custom-call(bf16[32,256]{1,0:T(8,128)(2,1)} %og_h.1, bf16[32,256]{1,0:T(8,128)(2,1)} %ig_h.1, bf16[32,256]{1,0:T(8,128)(2,1)} %va_h.1, bf16[32,256]{1,0:T(8,128)(2,1)} %go_h.1, ...), custom_call_target="tpu_custom_call" | custom-call | tf_op jit(solution)/shard_map/pallas_call | solution.py:445
  25.7 0.7 %shard_map.156 = (bf16[32,256]{1,0:T(8,128)(2,1)}, bf16[32,256]{1,0:T(8,128)(2,1)}, bf16[32,256]{1,0:T(8,128)(2,1)}, f32[4,256]{1,0:T(4,128)}, f32[32,128]{1,0:T(8,128)}) custom-call(bf16[32,256]{1,0:T(8,128)(2,1)S(1)} %get-tuple-element.10.a, bf16[32,256]{1,0:T(8,128)(2,1)S(1)} %get-tuple-element.11.b, bf16[32,256]{1,0:T(8,128)(2,1)S(1)} %get-tuple-element.12.c, ...), custom_call_target="tpu_custom_call" | custom-call | tf_op jit(solution)/shard_map/pallas_call | solution.py:471

commit v7 on v6

--- a/solution.py
+++ b/solution.py
@@ -14,7 +14,7 @@
 bf16 = jnp.bfloat16
 N = 16384
 LEAD = 12
-DIRECT = 2
+DIRECT = 0
 TOLD = 4
 VMEM_BYTES = 16 * 1024 * 1024
 W = 128
@@ -89,11 +89,11 @@
     *[(0, 0), (0, 1), (1, 0), (3, 0)],
     *[(1, 1), (3, 1), (2, 0), (2, 1)],
     *[(0, 7), (0, 2), (1, 2), (0, 3)],
-    *[(1, 7), (3, 7), (0, 6), (3, 2)],
-    *[(0, 5), (0, 4), (2, 5), (2, 4)],
-    *[(3, 6), (3, 3), (2, 6), (3, 4)],
-    *[(1, 6), (1, 3), (3, 5), (1, 4)],
-    *[(2, 7), (2, 2), (1, 5), (2, 3)],
+    *[(1, 3), (1, 7), (0, 6), (3, 2)],
+    *[(0, 5), (2, 7), (0, 4), (2, 6)],
+    *[(1, 6), (3, 3), (2, 3), (3, 5)],
+    *[(2, 2), (3, 7), (1, 5), (3, 6)],
+    *[(1, 4), (2, 5), (3, 4), (2, 4)],
 ]
 
 

time: 26.7 us -> 26.6 us (level)
  no operation moved by 1% of the time
where the time goes in v7:
time: 26.6 us; the launch traced here: 26.4 us
  Pallas kernels  25.7 us (97%)
  between operations  0.64 us (2%)
    pallas_call x1, Pallas kernels, local(): pl.pallas_call(kernel, out_shape=[*[vm(*o) for o in outs], vm((32, 2, W),...  25 us
    pallas_call x1, Pallas kernels, local(): pl.pallas_call(deliver, out_shape=[*shapes[:3], jax.ShapeDtypeStruct((4,...  0.67 us

profile of v7, /device:TPU:1, one launch (start us, length us, event | category | flops | bytes accessed | tf_op | source)
XLA Modules:
  0.0 26.4 jit_solution(3681806061689219524)
XLA Ops:
  0.6 25.0 %shard_map.155 = (bf16[32,256]{1,0:T(8,128)(2,1)S(1)}, bf16[32,256]{1,0:T(8,128)(2,1)S(1)}, bf16[32,256]{1,0:T(8,128)(2,1)S(1)}, f32[32,128]{1,0:T(8,128)S(1)}, f32[32,2,128]{2,1,0:T(2,128)S(1)}) custom-call(bf16[32,256]{1,0:T(8,128)(2,1)} %og_h.1, bf16[32,256]{1,0:T(8,128)(2,1)} %ig_h.1, bf16[32,256]{1,0:T(8,128)(2,1)} %va_h.1, bf16[32,256]{1,0:T(8,128)(2,1)} %go_h.1, ...), custom_call_target="tpu_custom_call" | custom-call | tf_op jit(solution)/shard_map/pallas_call | solution.py:445
  25.7 0.7 %shard_map.156 = (bf16[32,256]{1,0:T(8,128)(2,1)}, bf16[32,256]{1,0:T(8,128)(2,1)}, bf16[32,256]{1,0:T(8,128)(2,1)}, f32[4,256]{1,0:T(4,128)}, f32[32,128]{1,0:T(8,128)}) custom-call(bf16[32,256]{1,0:T(8,128)(2,1)S(1)} %get-tuple-element.10.a, bf16[32,256]{1,0:T(8,128)(2,1)S(1)} %get-tuple-element.11.b, bf16[32,256]{1,0:T(8,128)(2,1)S(1)} %get-tuple-element.12.c, ...), custom_call_target="tpu_custom_call" | custom-call | tf_op jit(solution)/shard_map/pallas_call | solution.py:471
